TPU v7x, 256 devices: a whole 4x4x8 slice. The times are simulated.
256 devices in a mesh: ctx: 32 (over x_hi, z, core), head: 8 (over y, x_lo).
Axes of the slice: x: 4 (x_hi: 2, x_lo: 2; x = x_hi * 2 + x_lo), y: 4, z: 8, core: 2. Of those that a mesh axis runs over, the one named last changes fastest.
Arguments:
- queries: bfloat16 [4, 2048, 8192], P(None, 'ctx', 'head'), as said below
- key_vectors: bfloat16 [4, 2048, 1024], P(None, 'ctx', 'head'), as said below
- value_vectors: bfloat16 [4, 2048, 1024], P(None, 'ctx', 'head'), may hold values from -6 to 6
- output_gradient: bfloat16 [4, 2048, 8192], P(None, 'ctx', 'head'), may hold values from -6 to 6
- positions: int32 [4, 2048], P(None, 'ctx'), may hold values from 0 to 2047, as said below
- segments: int32 [4, 2048], P(None, 'ctx'), may hold values from 0 to 7, as said below
Outputs:
- query_grad: bfloat16 [4, 2048, 8192], P(None, ('ctx', 'head'))
- key_gradient: bfloat16 [4, 2048, 1024], P(None, ('ctx', 'head'))
- value_gradient: bfloat16 [4, 2048, 1024], P(None, ('ctx', 'head'))
Inputs may be any that keep to these rules, and one draw needn't show every extreme that they name: `positions`: in each window each position appears in exactly one row. `segments`: in each window documents are runs of consecutive positions numbered in order of position, and every id of the range is used. `queries`: real-valued. `key_vectors`: real-valued.
All inputs are finite; a program needn't handle non-finite values.
Results may differ from a plain program's by a relative error of at most 0.012.
Values may be sent and summed in bfloat16 or wider, within the bound.
No kernel may reach another device: no remote copies, remote signals or barrier semaphores. Data moves between devices by JAX's collectives and lax.ppermute only.
A program may use at most 64 MiB of HBM per device.

v0:
```python
import math
import jax
import jax.numpy as jnp
from jax import lax
from jax.sharding import PartitionSpec as P

QUERY_HEADS = 64
KEY_VALUE_HEADS = 8
HEAD_SIZE = 128
NEG_BIG = -1e30


def passed_along(array, axis, by):
    count = lax.axis_size(axis)
    return lax.ppermute(array, axis, [(i, (i + by) % count) for i in range(count)])


def block_scores(query_four_axes, key_block, key_pos, key_seg, query_pos, query_seg):
    key_per_head = key_block.shape[1] // HEAD_SIZE
    key_three = key_block.reshape(key_block.shape[0], key_per_head, HEAD_SIZE)
    scores = jnp.einsum(
        "tkgd,skd->kgts", query_four_axes, key_three, preferred_element_type=jnp.float32
    ) * (1.0 / math.sqrt(HEAD_SIZE))
    allowed = (query_seg[:, None] == key_seg[None, :]) & (key_pos[None, :] <= query_pos[:, None])
    return (jnp.where(allowed, scores, NEG_BIG), allowed, key_three)


def stats_update(state_now, pieces, query_four_axes, grad_four, query_pos, query_seg):
    running_max, running_sum, running_dot = state_now
    key_block, value_block, key_pos, key_seg = pieces
    scores, allowed, key_three = block_scores(
        query_four_axes, key_block, key_pos, key_seg, query_pos, query_seg
    )
    value_three = value_block.reshape(key_three.shape)
    softmax_grad = jnp.einsum(
        "tkgd,skd->kgts", grad_four, value_three, preferred_element_type=jnp.float32
    )
    new_max = jnp.maximum(running_max, jnp.max(scores, axis=-1, keepdims=True))
    rescale = jnp.exp(running_max - new_max)
    weights = jnp.where(allowed, jnp.exp(scores - new_max), 0.0)
    new_sum = running_sum * rescale + jnp.sum(weights, axis=-1, keepdims=True)
    new_dot = running_dot * rescale + jnp.sum(weights * softmax_grad, axis=-1, keepdims=True)
    return (new_max, new_sum, new_dot)


def block_grads(pieces, query_four_axes, grad_four, logsum, row_delta, query_pos, query_seg):
    key_block, value_block, key_pos, key_seg = pieces
    key_rows = key_block.shape[0]
    factor = 1.0 / math.sqrt(HEAD_SIZE)
    scores, allowed, key_three = block_scores(
        query_four_axes, key_block, key_pos, key_seg, query_pos, query_seg
    )
    value_three = value_block.reshape(key_three.shape)
    softmax_out = jnp.where(allowed, jnp.exp(scores - logsum), 0.0)
    softmax_grad = jnp.einsum(
        "tkgd,skd->kgts", grad_four, value_three, preferred_element_type=jnp.float32
    )
    score_grad = softmax_out * (softmax_grad - row_delta)
    softmax_low = softmax_out.astype(jnp.bfloat16)
    score_low = score_grad.astype(jnp.bfloat16)
    value_part = jnp.einsum(
        "kgts,tkgd->skd", softmax_low, grad_four, preferred_element_type=jnp.float32
    ).reshape(key_rows, key_block.shape[1])
    key_part = (
        jnp.einsum(
            "kgts,tkgd->skd", score_low, query_four_axes, preferred_element_type=jnp.float32
        ).reshape(key_rows, key_block.shape[1])
        * factor
    )
    query_part = (
        jnp.einsum("kgts,skd->tkgd", score_low, key_three, preferred_element_type=jnp.float32)
        * factor
    )
    return (query_part, key_part, value_part)


def on_device(queries, key_vectors, value_vectors, output_gradient, positions, segments):
    window_count = queries.shape[0]
    row_count = queries.shape[1]
    query_groups = QUERY_HEADS // KEY_VALUE_HEADS
    key_width = key_vectors.shape[2]
    key_per_head = key_width // HEAD_SIZE
    query_five = queries.reshape(window_count, row_count, key_per_head, query_groups, HEAD_SIZE)
    grad_five = output_gradient.reshape(
        window_count, row_count, key_per_head, query_groups, HEAD_SIZE
    )
    stat_shape = (window_count, key_per_head, query_groups, row_count, 1)
    start_stats = (
        jnp.full(stat_shape, NEG_BIG, jnp.float32),
        jnp.zeros(stat_shape, jnp.float32),
        jnp.zeros(stat_shape, jnp.float32),
    )
    query_zero = jnp.zeros(query_five.shape, jnp.float32)
    stats_many = jax.vmap(stats_update)
    grads_many = jax.vmap(block_grads)
    gathered = (
        lax.all_gather(key_vectors, "ctx", axis=1, tiled=True),
        lax.all_gather(value_vectors, "ctx", axis=1, tiled=True),
        lax.all_gather(positions, "ctx", axis=1, tiled=True),
        lax.all_gather(segments, "ctx", axis=1, tiled=True),
    )
    whole_rows = gathered[0].shape[1]
    per_block = row_count * math.gcd(lax.axis_size("ctx"), max(1, 512 // row_count))
    block_count = whole_rows // per_block
    blocked = tuple(
        (
            jnp.moveaxis(
                member.reshape((window_count, block_count, per_block) + member.shape[2:]), 1, 0
            )
            for member in gathered
        )
    )

    def stats_step(state_now, pieces):
        return (stats_many(state_now, pieces, query_five, grad_five, positions, segments), None)

    (running_max, running_sum, running_dot), unused = lax.scan(stats_step, start_stats, blocked)
    logsum = running_max + jnp.log(running_sum)
    row_delta = running_dot / running_sum
    circle_size = lax.axis_size("ctx")
    own_index = lax.axis_index("ctx")
    key_zero = jnp.zeros(key_vectors.shape, jnp.float32)

    def cycle_turn(turn_index, cycle_state):
        query_acc, key_acc, value_acc = cycle_state
        source = (own_index - turn_index) % circle_size
        start_row = source * row_count
        pieces = tuple(
            (lax.dynamic_slice_in_dim(member, start_row, row_count, 1) for member in gathered)
        )
        query_part, key_part, value_part = grads_many(
            pieces, query_five, grad_five, logsum, row_delta, positions, segments
        )
        key_acc, value_acc = passed_along((key_acc + key_part, value_acc + value_part), "ctx", 1)
        return (query_acc + query_part, key_acc, value_acc)

    query_acc, key_acc, value_acc = lax.fori_loop(
        0, circle_size, cycle_turn, (query_zero, key_zero, key_zero)
    )
    query_low = query_acc.reshape(window_count, row_count, queries.shape[2]).astype(jnp.bfloat16)
    key_low = key_acc.astype(jnp.bfloat16)
    value_low = value_acc.astype(jnp.bfloat16)
    query_grad, key_gradient, value_gradient = (
        lax.all_to_all(query_low, "head", split_axis=1, concat_axis=2, tiled=True),
        lax.all_to_all(key_low, "head", split_axis=1, concat_axis=2, tiled=True),
        lax.all_to_all(value_low, "head", split_axis=1, concat_axis=2, tiled=True),
    )
    return (query_grad, key_gradient, value_gradient)


def solution(mesh):
    return jax.shard_map(
        on_device,
        mesh=mesh,
        in_specs=(
            P(None, "ctx", "head"),
            P(None, "ctx", "head"),
            P(None, "ctx", "head"),
            P(None, "ctx", "head"),
            P(None, "ctx"),
            P(None, "ctx"),
        ),
        out_specs=(
            P(None, ("ctx", "head"), None),
            P(None, ("ctx", "head"), None),
            P(None, ("ctx", "head"), None),
        ),
        check_vma=False,
    )
```

profile of v0, /device:TPU:2, one launch (start us, length us, event | category | flops | bytes accessed | tf_op | source)
XLA Modules:
  0.0 674.8 jit_solution(3938459747164289178)
XLA Ops:
  11.3 44.0 %all-gather = s32[32,64,4]{1,2,0:T(4,128)S(1)} all-gather(s32[1,64,4]{1,2,0:T(4,128)S(1)} %bitcast.257), channel_id=1, replica_groups=mesh['ctx'=32,'head'=8] {'ctx'}, dimensions={0}, use_global_device_ids=true | all-gather | bytes 33792 | tf_op jit(solution)/shard_map/all_gather | solution.py:100
  55.3 37.0 %all-gather.1 = s32[32,64,4]{1,2,0:T(4,128)S(1)} all-gather(s32[1,64,4]{1,2,0:T(4,128)S(1)} %bitcast.258), channel_id=1, replica_groups=mesh['ctx'=32,'head'=8] {'ctx'}, dimensions={0}, use_global_device_ids=true | all-gather | bytes 33792 | tf_op jit(solution)/shard_map/all_gather | solution.py:99
  92.9 3.1 copy.81
  96.1 76.3 %all-gather.5.cloned.1.call-done = bf16[4,2048,128]{2,1,0:T(8,128)(2,1)} async-done(((bf16[4,64,128]{2,1,0:T(8,128)(2,1)}), bf16[4,2048,128]{2,1,0:T(8,128)(2,1)}) %all-gather.5.cloned.1.call-update) | async-done | bytes 2097168 | tf_op jit(solution)/shard_map/all_gather | solution.py:97
  172.4 3.2 copy.82
  175.6 42.4 %while.35 = (s32[]{:T(128)}, f32[4,1,8,64,1]{3,2,0,4,1:T(8,128)S(1)}, f32[4,1,8,64,1]{3,2,0,4,1:T(8,128)S(1)}, f32[4,1,8,64,1]{3,2,0,4,1:T(8,128)S(1)}, s32[4,64...) while((s32[]{:T(128)}, ...), condition=%wide.region_4.5_spmd.clone, body=%wide.region_0.4_spmd.clone.sunk | while | flops 551958528 | bytes 32181424 | solution.py:117
  175.8 3.8 fusion.66
  179.5 3.7 fusion.68
  183.2 2.9 fusion.67
  186.4 3.8 fusion.66
  190.1 3.7 fusion.68
  193.8 2.9 fusion.67
  197.0 3.8 fusion.66
  200.7 3.7 fusion.68
  204.4 2.9 fusion.67
  207.6 3.8 fusion.66
  211.4 3.7 fusion.68
  215.1 2.9 fusion.67
  218.1 415.3 %while.36 = (s32[]{:T(128)}, f32[4,64,1,8,128]{4,1,3,0,2:T(8,128)S(1)}, f32[4,64,128]{2,1,0:T(8,128)S(1)}, f32[4,64,128]{2,1,0:T(8,128)S(1)}, s32[]{:T(128)}, /*...) while((s32[]{:T(128)}, ...), condition=%wide.region_6.7_spmd.clone, body=%wide.region_5.6_spmd.clone.sunk | while | flops 169754640 | bytes 8380878 | solution.py:137
  224.2 5.4 collective-permute-done
  231.3 1.5 fusion.79
  236.4 6.3 collective-permute-done
  249.3 6.3 collective-permute-done
  262.3 6.3 collective-permute-done
  270.2 1.5 fusion.79
  275.3 6.3 collective-permute-done
  283.2 1.5 fusion.79
  288.3 6.3 collective-permute-done
  296.2 1.5 fusion.79
  301.2 6.3 collective-permute-done
  309.2 1.5 fusion.79
  314.2 6.3 collective-permute-done
  322.1 1.5 fusion.79
  327.2 6.3 collective-permute-done
  335.1 1.5 fusion.79
  340.2 6.3 collective-permute-done
  353.2 6.3 collective-permute-done
  366.1 6.3 collective-permute-done
  379.1 6.3 collective-permute-done
  392.1 6.3 collective-permute-done
  405.1 6.3 collective-permute-done
  418.0 6.3 collective-permute-done
  431.0 6.3 collective-permute-done
  444.0 6.3 collective-permute-done
  457.0 6.3 collective-permute-done
  469.9 6.3 collective-permute-done
  482.9 6.3 collective-permute-done
  495.9 6.3 collective-permute-done
  508.9 6.3 collective-permute-done
  521.9 6.3 collective-permute-done
  534.8 6.3 collective-permute-done
  547.8 6.3 collective-permute-done
  560.8 6.3 collective-permute-done
  573.8 6.3 collective-permute-done
  586.7 6.3 collective-permute-done
  599.7 6.3 collective-permute-done
  612.7 6.3 collective-permute-done
  625.7 6.3 collective-permute-done
  634.1 5.7 all-to-all-start.2
  640.5 4.3 all-to-all-done.2
  644.9 4.5 all-to-all-start.1
  650.8 4.7 all-to-all-done.1
  655.5 4.0 all-to-all-start
  660.8 6.3 all-to-all-done
  (373 shorter events, 213.1 us)
Async XLA Ops:
  7.2 85.8 %all-gather.7.cloned.1.call-start = ((), (), s32[]{:S(2)}) async-start(), calls=%async_computation.4 | async-start | bytes 2162688 | tf_op jit(solution)/shard_map/all_gather | solution.py:98
  7.9 164.5 %all-gather.5.cloned.1.call-start = ((), (), s32[]{:S(2)}) async-start(), calls=%async_computation.3 | async-start | bytes 2162688 | tf_op jit(solution)/shard_map/all_gather | solution.py:97
  221.6 8.1 %collective-permute-start = (f32[4,64,128]{2,1,0:T(8,128)S(1)}, f32[4,64,128]{2,1,0:T(8,128)S(1)}, u32[]{:S(2)}, u32[]{:S(2)}) collective-permute-start(f32[4,64,128]{2,1,0:T(8,128)S(1)} %fusion.82), channel_id=1, source_target_pairs={{0,8},{8,16},{16,24},{24,32},{32,40},{40,48},{48,56},{56,64},{64,7... | collective-permute-start | bytes 393224 | tf_op jit(solution)/shard_map/while/body/eval_jaxpr/ppermute | solution.py:15
  222.2 8.9 %collective-permute-start.1 = (f32[4,64,128]{2,1,0:T(8,128)S(1)}, f32[4,64,128]{2,1,0:T(8,128)S(1)}, u32[]{:S(2)}, u32[]{:S(2)}) collective-permute-start(f32[4,64,128]{2,1,0:T(8,128)S(1)} %fusion.83), channel_id=1, source_target_pairs={{0,8},{8,16},{16,24},{24,32},{32,40},{40,48},{48,56},{56,64},{64,7... | collective-permute-start | bytes 393224 | tf_op jit(solution)/shard_map/while/body/eval_jaxpr/ppermute | solution.py:15
  234.6 8.1 %collective-permute-start = (f32[4,64,128]{2,1,0:T(8,128)S(1)}, f32[4,64,128]{2,1,0:T(8,128)S(1)}, u32[]{:S(2)}, u32[]{:S(2)}) collective-permute-start(f32[4,64,128]{2,1,0:T(8,128)S(1)} %fusion.82), channel_id=1, source_target_pairs={{0,8},{8,16},{16,24},{24,32},{32,40},{40,48},{48,56},{56,64},{64,7... | collective-permute-start | bytes 393224 | tf_op jit(solution)/shard_map/while/body/eval_jaxpr/ppermute | solution.py:15
  234.9 9.1 %collective-permute-start.1 = (f32[4,64,128]{2,1,0:T(8,128)S(1)}, f32[4,64,128]{2,1,0:T(8,128)S(1)}, u32[]{:S(2)}, u32[]{:S(2)}) collective-permute-start(f32[4,64,128]{2,1,0:T(8,128)S(1)} %fusion.83), channel_id=1, source_target_pairs={{0,8},{8,16},{16,24},{24,32},{32,40},{40,48},{48,56},{56,64},{64,7... | collective-permute-start | bytes 393224 | tf_op jit(solution)/shard_map/while/body/eval_jaxpr/ppermute | solution.py:15
  247.5 8.1 %collective-permute-start = (f32[4,64,128]{2,1,0:T(8,128)S(1)}, f32[4,64,128]{2,1,0:T(8,128)S(1)}, u32[]{:S(2)}, u32[]{:S(2)}) collective-permute-start(f32[4,64,128]{2,1,0:T(8,128)S(1)} %fusion.82), channel_id=1, source_target_pairs={{0,8},{8,16},{16,24},{24,32},{32,40},{40,48},{48,56},{56,64},{64,7... | collective-permute-start | bytes 393224 | tf_op jit(solution)/shard_map/while/body/eval_jaxpr/ppermute | solution.py:15
  247.9 9.1 %collective-permute-start.1 = (f32[4,64,128]{2,1,0:T(8,128)S(1)}, f32[4,64,128]{2,1,0:T(8,128)S(1)}, u32[]{:S(2)}, u32[]{:S(2)}) collective-permute-start(f32[4,64,128]{2,1,0:T(8,128)S(1)} %fusion.83), channel_id=1, source_target_pairs={{0,8},{8,16},{16,24},{24,32},{32,40},{40,48},{48,56},{56,64},{64,7... | collective-permute-start | bytes 393224 | tf_op jit(solution)/shard_map/while/body/eval_jaxpr/ppermute | solution.py:15
  260.5 8.1 %collective-permute-start = (f32[4,64,128]{2,1,0:T(8,128)S(1)}, f32[4,64,128]{2,1,0:T(8,128)S(1)}, u32[]{:S(2)}, u32[]{:S(2)}) collective-permute-start(f32[4,64,128]{2,1,0:T(8,128)S(1)} %fusion.82), channel_id=1, source_target_pairs={{0,8},{8,16},{16,24},{24,32},{32,40},{40,48},{48,56},{56,64},{64,7... | collective-permute-start | bytes 393224 | tf_op jit(solution)/shard_map/while/body/eval_jaxpr/ppermute | solution.py:15
  260.9 9.1 %collective-permute-start.1 = (f32[4,64,128]{2,1,0:T(8,128)S(1)}, f32[4,64,128]{2,1,0:T(8,128)S(1)}, u32[]{:S(2)}, u32[]{:S(2)}) collective-permute-start(f32[4,64,128]{2,1,0:T(8,128)S(1)} %fusion.83), channel_id=1, source_target_pairs={{0,8},{8,16},{16,24},{24,32},{32,40},{40,48},{48,56},{56,64},{64,7... | collective-permute-start | bytes 393224 | tf_op jit(solution)/shard_map/while/body/eval_jaxpr/ppermute | solution.py:15
  273.5 8.1 %collective-permute-start = (f32[4,64,128]{2,1,0:T(8,128)S(1)}, f32[4,64,128]{2,1,0:T(8,128)S(1)}, u32[]{:S(2)}, u32[]{:S(2)}) collective-permute-start(f32[4,64,128]{2,1,0:T(8,128)S(1)} %fusion.82), channel_id=1, source_target_pairs={{0,8},{8,16},{16,24},{24,32},{32,40},{40,48},{48,56},{56,64},{64,7... | collective-permute-start | bytes 393224 | tf_op jit(solution)/shard_map/while/body/eval_jaxpr/ppermute | solution.py:15
  273.9 9.1 %collective-permute-start.1 = (f32[4,64,128]{2,1,0:T(8,128)S(1)}, f32[4,64,128]{2,1,0:T(8,128)S(1)}, u32[]{:S(2)}, u32[]{:S(2)}) collective-permute-start(f32[4,64,128]{2,1,0:T(8,128)S(1)} %fusion.83), channel_id=1, source_target_pairs={{0,8},{8,16},{16,24},{24,32},{32,40},{40,48},{48,56},{56,64},{64,7... | collective-permute-start | bytes 393224 | tf_op jit(solution)/shard_map/while/body/eval_jaxpr/ppermute | solution.py:15
  286.5 8.1 %collective-permute-start = (f32[4,64,128]{2,1,0:T(8,128)S(1)}, f32[4,64,128]{2,1,0:T(8,128)S(1)}, u32[]{:S(2)}, u32[]{:S(2)}) collective-permute-start(f32[4,64,128]{2,1,0:T(8,128)S(1)} %fusion.82), channel_id=1, source_target_pairs={{0,8},{8,16},{16,24},{24,32},{32,40},{40,48},{48,56},{56,64},{64,7... | collective-permute-start | bytes 393224 | tf_op jit(solution)/shard_map/while/body/eval_jaxpr/ppermute | solution.py:15
  286.9 9.1 %collective-permute-start.1 = (f32[4,64,128]{2,1,0:T(8,128)S(1)}, f32[4,64,128]{2,1,0:T(8,128)S(1)}, u32[]{:S(2)}, u32[]{:S(2)}) collective-permute-start(f32[4,64,128]{2,1,0:T(8,128)S(1)} %fusion.83), channel_id=1, source_target_pairs={{0,8},{8,16},{16,24},{24,32},{32,40},{40,48},{48,56},{56,64},{64,7... | collective-permute-start | bytes 393224 | tf_op jit(solution)/shard_map/while/body/eval_jaxpr/ppermute | solution.py:15
  299.4 8.1 %collective-permute-start = (f32[4,64,128]{2,1,0:T(8,128)S(1)}, f32[4,64,128]{2,1,0:T(8,128)S(1)}, u32[]{:S(2)}, u32[]{:S(2)}) collective-permute-start(f32[4,64,128]{2,1,0:T(8,128)S(1)} %fusion.82), channel_id=1, source_target_pairs={{0,8},{8,16},{16,24},{24,32},{32,40},{40,48},{48,56},{56,64},{64,7... | collective-permute-start | bytes 393224 | tf_op jit(solution)/shard_map/while/body/eval_jaxpr/ppermute | solution.py:15
  299.8 9.1 %collective-permute-start.1 = (f32[4,64,128]{2,1,0:T(8,128)S(1)}, f32[4,64,128]{2,1,0:T(8,128)S(1)}, u32[]{:S(2)}, u32[]{:S(2)}) collective-permute-start(f32[4,64,128]{2,1,0:T(8,128)S(1)} %fusion.83), channel_id=1, source_target_pairs={{0,8},{8,16},{16,24},{24,32},{32,40},{40,48},{48,56},{56,64},{64,7... | collective-permute-start | bytes 393224 | tf_op jit(solution)/shard_map/while/body/eval_jaxpr/ppermute | solution.py:15
  312.4 8.1 %collective-permute-start = (f32[4,64,128]{2,1,0:T(8,128)S(1)}, f32[4,64,128]{2,1,0:T(8,128)S(1)}, u32[]{:S(2)}, u32[]{:S(2)}) collective-permute-start(f32[4,64,128]{2,1,0:T(8,128)S(1)} %fusion.82), channel_id=1, source_target_pairs={{0,8},{8,16},{16,24},{24,32},{32,40},{40,48},{48,56},{56,64},{64,7... | collective-permute-start | bytes 393224 | tf_op jit(solution)/shard_map/while/body/eval_jaxpr/ppermute | solution.py:15
  312.8 9.1 %collective-permute-start.1 = (f32[4,64,128]{2,1,0:T(8,128)S(1)}, f32[4,64,128]{2,1,0:T(8,128)S(1)}, u32[]{:S(2)}, u32[]{:S(2)}) collective-permute-start(f32[4,64,128]{2,1,0:T(8,128)S(1)} %fusion.83), channel_id=1, source_target_pairs={{0,8},{8,16},{16,24},{24,32},{32,40},{40,48},{48,56},{56,64},{64,7... | collective-permute-start | bytes 393224 | tf_op jit(solution)/shard_map/while/body/eval_jaxpr/ppermute | solution.py:15
  325.4 8.1 %collective-permute-start = (f32[4,64,128]{2,1,0:T(8,128)S(1)}, f32[4,64,128]{2,1,0:T(8,128)S(1)}, u32[]{:S(2)}, u32[]{:S(2)}) collective-permute-start(f32[4,64,128]{2,1,0:T(8,128)S(1)} %fusion.82), channel_id=1, source_target_pairs={{0,8},{8,16},{16,24},{24,32},{32,40},{40,48},{48,56},{56,64},{64,7... | collective-permute-start | bytes 393224 | tf_op jit(solution)/shard_map/while/body/eval_jaxpr/ppermute | solution.py:15
  325.8 9.1 %collective-permute-start.1 = (f32[4,64,128]{2,1,0:T(8,128)S(1)}, f32[4,64,128]{2,1,0:T(8,128)S(1)}, u32[]{:S(2)}, u32[]{:S(2)}) collective-permute-start(f32[4,64,128]{2,1,0:T(8,128)S(1)} %fusion.83), channel_id=1, source_target_pairs={{0,8},{8,16},{16,24},{24,32},{32,40},{40,48},{48,56},{56,64},{64,7... | collective-permute-start | bytes 393224 | tf_op jit(solution)/shard_map/while/body/eval_jaxpr/ppermute | solution.py:15
  338.4 8.1 %collective-permute-start = (f32[4,64,128]{2,1,0:T(8,128)S(1)}, f32[4,64,128]{2,1,0:T(8,128)S(1)}, u32[]{:S(2)}, u32[]{:S(2)}) collective-permute-start(f32[4,64,128]{2,1,0:T(8,128)S(1)} %fusion.82), channel_id=1, source_target_pairs={{0,8},{8,16},{16,24},{24,32},{32,40},{40,48},{48,56},{56,64},{64,7... | collective-permute-start | bytes 393224 | tf_op jit(solution)/shard_map/while/body/eval_jaxpr/ppermute | solution.py:15
  338.8 9.1 %collective-permute-start.1 = (f32[4,64,128]{2,1,0:T(8,128)S(1)}, f32[4,64,128]{2,1,0:T(8,128)S(1)}, u32[]{:S(2)}, u32[]{:S(2)}) collective-permute-start(f32[4,64,128]{2,1,0:T(8,128)S(1)} %fusion.83), channel_id=1, source_target_pairs={{0,8},{8,16},{16,24},{24,32},{32,40},{40,48},{48,56},{56,64},{64,7... | collective-permute-start | bytes 393224 | tf_op jit(solution)/shard_map/while/body/eval_jaxpr/ppermute | solution.py:15
  351.4 8.1 %collective-permute-start = (f32[4,64,128]{2,1,0:T(8,128)S(1)}, f32[4,64,128]{2,1,0:T(8,128)S(1)}, u32[]{:S(2)}, u32[]{:S(2)}) collective-permute-start(f32[4,64,128]{2,1,0:T(8,128)S(1)} %fusion.82), channel_id=1, source_target_pairs={{0,8},{8,16},{16,24},{24,32},{32,40},{40,48},{48,56},{56,64},{64,7... | collective-permute-start | bytes 393224 | tf_op jit(solution)/shard_map/while/body/eval_jaxpr/ppermute | solution.py:15
  351.7 9.1 %collective-permute-start.1 = (f32[4,64,128]{2,1,0:T(8,128)S(1)}, f32[4,64,128]{2,1,0:T(8,128)S(1)}, u32[]{:S(2)}, u32[]{:S(2)}) collective-permute-start(f32[4,64,128]{2,1,0:T(8,128)S(1)} %fusion.83), channel_id=1, source_target_pairs={{0,8},{8,16},{16,24},{24,32},{32,40},{40,48},{48,56},{56,64},{64,7... | collective-permute-start | bytes 393224 | tf_op jit(solution)/shard_map/while/body/eval_jaxpr/ppermute | solution.py:15
  364.3 8.1 %collective-permute-start = (f32[4,64,128]{2,1,0:T(8,128)S(1)}, f32[4,64,128]{2,1,0:T(8,128)S(1)}, u32[]{:S(2)}, u32[]{:S(2)}) collective-permute-start(f32[4,64,128]{2,1,0:T(8,128)S(1)} %fusion.82), channel_id=1, source_target_pairs={{0,8},{8,16},{16,24},{24,32},{32,40},{40,48},{48,56},{56,64},{64,7... | collective-permute-start | bytes 393224 | tf_op jit(solution)/shard_map/while/body/eval_jaxpr/ppermute | solution.py:15
  364.7 9.1 %collective-permute-start.1 = (f32[4,64,128]{2,1,0:T(8,128)S(1)}, f32[4,64,128]{2,1,0:T(8,128)S(1)}, u32[]{:S(2)}, u32[]{:S(2)}) collective-permute-start(f32[4,64,128]{2,1,0:T(8,128)S(1)} %fusion.83), channel_id=1, source_target_pairs={{0,8},{8,16},{16,24},{24,32},{32,40},{40,48},{48,56},{56,64},{64,7... | collective-permute-start | bytes 393224 | tf_op jit(solution)/shard_map/while/body/eval_jaxpr/ppermute | solution.py:15
  377.3 8.1 %collective-permute-start = (f32[4,64,128]{2,1,0:T(8,128)S(1)}, f32[4,64,128]{2,1,0:T(8,128)S(1)}, u32[]{:S(2)}, u32[]{:S(2)}) collective-permute-start(f32[4,64,128]{2,1,0:T(8,128)S(1)} %fusion.82), channel_id=1, source_target_pairs={{0,8},{8,16},{16,24},{24,32},{32,40},{40,48},{48,56},{56,64},{64,7... | collective-permute-start | bytes 393224 | tf_op jit(solution)/shard_map/while/body/eval_jaxpr/ppermute | solution.py:15
  377.7 9.1 %collective-permute-start.1 = (f32[4,64,128]{2,1,0:T(8,128)S(1)}, f32[4,64,128]{2,1,0:T(8,128)S(1)}, u32[]{:S(2)}, u32[]{:S(2)}) collective-permute-start(f32[4,64,128]{2,1,0:T(8,128)S(1)} %fusion.83), channel_id=1, source_target_pairs={{0,8},{8,16},{16,24},{24,32},{32,40},{40,48},{48,56},{56,64},{64,7... | collective-permute-start | bytes 393224 | tf_op jit(solution)/shard_map/while/body/eval_jaxpr/ppermute | solution.py:15
  390.3 8.1 %collective-permute-start = (f32[4,64,128]{2,1,0:T(8,128)S(1)}, f32[4,64,128]{2,1,0:T(8,128)S(1)}, u32[]{:S(2)}, u32[]{:S(2)}) collective-permute-start(f32[4,64,128]{2,1,0:T(8,128)S(1)} %fusion.82), channel_id=1, source_target_pairs={{0,8},{8,16},{16,24},{24,32},{32,40},{40,48},{48,56},{56,64},{64,7... | collective-permute-start | bytes 393224 | tf_op jit(solution)/shard_map/while/body/eval_jaxpr/ppermute | solution.py:15
  390.7 9.1 %collective-permute-start.1 = (f32[4,64,128]{2,1,0:T(8,128)S(1)}, f32[4,64,128]{2,1,0:T(8,128)S(1)}, u32[]{:S(2)}, u32[]{:S(2)}) collective-permute-start(f32[4,64,128]{2,1,0:T(8,128)S(1)} %fusion.83), channel_id=1, source_target_pairs={{0,8},{8,16},{16,24},{24,32},{32,40},{40,48},{48,56},{56,64},{64,7... | collective-permute-start | bytes 393224 | tf_op jit(solution)/shard_map/while/body/eval_jaxpr/ppermute | solution.py:15
  403.3 8.1 %collective-permute-start = (f32[4,64,128]{2,1,0:T(8,128)S(1)}, f32[4,64,128]{2,1,0:T(8,128)S(1)}, u32[]{:S(2)}, u32[]{:S(2)}) collective-permute-start(f32[4,64,128]{2,1,0:T(8,128)S(1)} %fusion.82), channel_id=1, source_target_pairs={{0,8},{8,16},{16,24},{24,32},{32,40},{40,48},{48,56},{56,64},{64,7... | collective-permute-start | bytes 393224 | tf_op jit(solution)/shard_map/while/body/eval_jaxpr/ppermute | solution.py:15
  403.6 9.1 %collective-permute-start.1 = (f32[4,64,128]{2,1,0:T(8,128)S(1)}, f32[4,64,128]{2,1,0:T(8,128)S(1)}, u32[]{:S(2)}, u32[]{:S(2)}) collective-permute-start(f32[4,64,128]{2,1,0:T(8,128)S(1)} %fusion.83), channel_id=1, source_target_pairs={{0,8},{8,16},{16,24},{24,32},{32,40},{40,48},{48,56},{56,64},{64,7... | collective-permute-start | bytes 393224 | tf_op jit(solution)/shard_map/while/body/eval_jaxpr/ppermute | solution.py:15
  416.2 8.1 %collective-permute-start = (f32[4,64,128]{2,1,0:T(8,128)S(1)}, f32[4,64,128]{2,1,0:T(8,128)S(1)}, u32[]{:S(2)}, u32[]{:S(2)}) collective-permute-start(f32[4,64,128]{2,1,0:T(8,128)S(1)} %fusion.82), channel_id=1, source_target_pairs={{0,8},{8,16},{16,24},{24,32},{32,40},{40,48},{48,56},{56,64},{64,7... | collective-permute-start | bytes 393224 | tf_op jit(solution)/shard_map/while/body/eval_jaxpr/ppermute | solution.py:15
  416.6 9.1 %collective-permute-start.1 = (f32[4,64,128]{2,1,0:T(8,128)S(1)}, f32[4,64,128]{2,1,0:T(8,128)S(1)}, u32[]{:S(2)}, u32[]{:S(2)}) collective-permute-start(f32[4,64,128]{2,1,0:T(8,128)S(1)} %fusion.83), channel_id=1, source_target_pairs={{0,8},{8,16},{16,24},{24,32},{32,40},{40,48},{48,56},{56,64},{64,7... | collective-permute-start | bytes 393224 | tf_op jit(solution)/shard_map/while/body/eval_jaxpr/ppermute | solution.py:15
  429.2 8.1 %collective-permute-start = (f32[4,64,128]{2,1,0:T(8,128)S(1)}, f32[4,64,128]{2,1,0:T(8,128)S(1)}, u32[]{:S(2)}, u32[]{:S(2)}) collective-permute-start(f32[4,64,128]{2,1,0:T(8,128)S(1)} %fusion.82), channel_id=1, source_target_pairs={{0,8},{8,16},{16,24},{24,32},{32,40},{40,48},{48,56},{56,64},{64,7... | collective-permute-start | bytes 393224 | tf_op jit(solution)/shard_map/while/body/eval_jaxpr/ppermute | solution.py:15
  429.6 9.1 %collective-permute-start.1 = (f32[4,64,128]{2,1,0:T(8,128)S(1)}, f32[4,64,128]{2,1,0:T(8,128)S(1)}, u32[]{:S(2)}, u32[]{:S(2)}) collective-permute-start(f32[4,64,128]{2,1,0:T(8,128)S(1)} %fusion.83), channel_id=1, source_target_pairs={{0,8},{8,16},{16,24},{24,32},{32,40},{40,48},{48,56},{56,64},{64,7... | collective-permute-start | bytes 393224 | tf_op jit(solution)/shard_map/while/body/eval_jaxpr/ppermute | solution.py:15
  442.2 8.1 %collective-permute-start = (f32[4,64,128]{2,1,0:T(8,128)S(1)}, f32[4,64,128]{2,1,0:T(8,128)S(1)}, u32[]{:S(2)}, u32[]{:S(2)}) collective-permute-start(f32[4,64,128]{2,1,0:T(8,128)S(1)} %fusion.82), channel_id=1, source_target_pairs={{0,8},{8,16},{16,24},{24,32},{32,40},{40,48},{48,56},{56,64},{64,7... | collective-permute-start | bytes 393224 | tf_op jit(solution)/shard_map/while/body/eval_jaxpr/ppermute | solution.py:15
  442.6 9.1 %collective-permute-start.1 = (f32[4,64,128]{2,1,0:T(8,128)S(1)}, f32[4,64,128]{2,1,0:T(8,128)S(1)}, u32[]{:S(2)}, u32[]{:S(2)}) collective-permute-start(f32[4,64,128]{2,1,0:T(8,128)S(1)} %fusion.83), channel_id=1, source_target_pairs={{0,8},{8,16},{16,24},{24,32},{32,40},{40,48},{48,56},{56,64},{64,7... | collective-permute-start | bytes 393224 | tf_op jit(solution)/shard_map/while/body/eval_jaxpr/ppermute | solution.py:15
  455.2 8.1 %collective-permute-start = (f32[4,64,128]{2,1,0:T(8,128)S(1)}, f32[4,64,128]{2,1,0:T(8,128)S(1)}, u32[]{:S(2)}, u32[]{:S(2)}) collective-permute-start(f32[4,64,128]{2,1,0:T(8,128)S(1)} %fusion.82), channel_id=1, source_target_pairs={{0,8},{8,16},{16,24},{24,32},{32,40},{40,48},{48,56},{56,64},{64,7... | collective-permute-start | bytes 393224 | tf_op jit(solution)/shard_map/while/body/eval_jaxpr/ppermute | solution.py:15
  455.5 9.1 %collective-permute-start.1 = (f32[4,64,128]{2,1,0:T(8,128)S(1)}, f32[4,64,128]{2,1,0:T(8,128)S(1)}, u32[]{:S(2)}, u32[]{:S(2)}) collective-permute-start(f32[4,64,128]{2,1,0:T(8,128)S(1)} %fusion.83), channel_id=1, source_target_pairs={{0,8},{8,16},{16,24},{24,32},{32,40},{40,48},{48,56},{56,64},{64,7... | collective-permute-start | bytes 393224 | tf_op jit(solution)/shard_map/while/body/eval_jaxpr/ppermute | solution.py:15
  468.1 8.1 %collective-permute-start = (f32[4,64,128]{2,1,0:T(8,128)S(1)}, f32[4,64,128]{2,1,0:T(8,128)S(1)}, u32[]{:S(2)}, u32[]{:S(2)}) collective-permute-start(f32[4,64,128]{2,1,0:T(8,128)S(1)} %fusion.82), channel_id=1, source_target_pairs={{0,8},{8,16},{16,24},{24,32},{32,40},{40,48},{48,56},{56,64},{64,7... | collective-permute-start | bytes 393224 | tf_op jit(solution)/shard_map/while/body/eval_jaxpr/ppermute | solution.py:15
  468.5 9.1 %collective-permute-start.1 = (f32[4,64,128]{2,1,0:T(8,128)S(1)}, f32[4,64,128]{2,1,0:T(8,128)S(1)}, u32[]{:S(2)}, u32[]{:S(2)}) collective-permute-start(f32[4,64,128]{2,1,0:T(8,128)S(1)} %fusion.83), channel_id=1, source_target_pairs={{0,8},{8,16},{16,24},{24,32},{32,40},{40,48},{48,56},{56,64},{64,7... | collective-permute-start | bytes 393224 | tf_op jit(solution)/shard_map/while/body/eval_jaxpr/ppermute | solution.py:15
  481.1 8.1 %collective-permute-start = (f32[4,64,128]{2,1,0:T(8,128)S(1)}, f32[4,64,128]{2,1,0:T(8,128)S(1)}, u32[]{:S(2)}, u32[]{:S(2)}) collective-permute-start(f32[4,64,128]{2,1,0:T(8,128)S(1)} %fusion.82), channel_id=1, source_target_pairs={{0,8},{8,16},{16,24},{24,32},{32,40},{40,48},{48,56},{56,64},{64,7... | collective-permute-start | bytes 393224 | tf_op jit(solution)/shard_map/while/body/eval_jaxpr/ppermute | solution.py:15
  481.5 9.1 %collective-permute-start.1 = (f32[4,64,128]{2,1,0:T(8,128)S(1)}, f32[4,64,128]{2,1,0:T(8,128)S(1)}, u32[]{:S(2)}, u32[]{:S(2)}) collective-permute-start(f32[4,64,128]{2,1,0:T(8,128)S(1)} %fusion.83), channel_id=1, source_target_pairs={{0,8},{8,16},{16,24},{24,32},{32,40},{40,48},{48,56},{56,64},{64,7... | collective-permute-start | bytes 393224 | tf_op jit(solution)/shard_map/while/body/eval_jaxpr/ppermute | solution.py:15
  494.1 8.1 %collective-permute-start = (f32[4,64,128]{2,1,0:T(8,128)S(1)}, f32[4,64,128]{2,1,0:T(8,128)S(1)}, u32[]{:S(2)}, u32[]{:S(2)}) collective-permute-start(f32[4,64,128]{2,1,0:T(8,128)S(1)} %fusion.82), channel_id=1, source_target_pairs={{0,8},{8,16},{16,24},{24,32},{32,40},{40,48},{48,56},{56,64},{64,7... | collective-permute-start | bytes 393224 | tf_op jit(solution)/shard_map/while/body/eval_jaxpr/ppermute | solution.py:15
  494.5 9.1 %collective-permute-start.1 = (f32[4,64,128]{2,1,0:T(8,128)S(1)}, f32[4,64,128]{2,1,0:T(8,128)S(1)}, u32[]{:S(2)}, u32[]{:S(2)}) collective-permute-start(f32[4,64,128]{2,1,0:T(8,128)S(1)} %fusion.83), channel_id=1, source_target_pairs={{0,8},{8,16},{16,24},{24,32},{32,40},{40,48},{48,56},{56,64},{64,7... | collective-permute-start | bytes 393224 | tf_op jit(solution)/shard_map/while/body/eval_jaxpr/ppermute | solution.py:15
  507.5 9.1 %collective-permute-start.1 = (f32[4,64,128]{2,1,0:T(8,128)S(1)}, f32[4,64,128]{2,1,0:T(8,128)S(1)}, u32[]{:S(2)}, u32[]{:S(2)}) collective-permute-start(f32[4,64,128]{2,1,0:T(8,128)S(1)} %fusion.83), channel_id=1, source_target_pairs={{0,8},{8,16},{16,24},{24,32},{32,40},{40,48},{48,56},{56,64},{64,7... | collective-permute-start | bytes 393224 | tf_op jit(solution)/shard_map/while/body/eval_jaxpr/ppermute | solution.py:15
  520.4 9.1 %collective-permute-start.1 = (f32[4,64,128]{2,1,0:T(8,128)S(1)}, f32[4,64,128]{2,1,0:T(8,128)S(1)}, u32[]{:S(2)}, u32[]{:S(2)}) collective-permute-start(f32[4,64,128]{2,1,0:T(8,128)S(1)} %fusion.83), channel_id=1, source_target_pairs={{0,8},{8,16},{16,24},{24,32},{32,40},{40,48},{48,56},{56,64},{64,7... | collective-permute-start | bytes 393224 | tf_op jit(solution)/shard_map/while/body/eval_jaxpr/ppermute | solution.py:15
  533.4 9.1 %collective-permute-start.1 = (f32[4,64,128]{2,1,0:T(8,128)S(1)}, f32[4,64,128]{2,1,0:T(8,128)S(1)}, u32[]{:S(2)}, u32[]{:S(2)}) collective-permute-start(f32[4,64,128]{2,1,0:T(8,128)S(1)} %fusion.83), channel_id=1, source_target_pairs={{0,8},{8,16},{16,24},{24,32},{32,40},{40,48},{48,56},{56,64},{64,7... | collective-permute-start | bytes 393224 | tf_op jit(solution)/shard_map/while/body/eval_jaxpr/ppermute | solution.py:15
  546.4 9.1 %collective-permute-start.1 = (f32[4,64,128]{2,1,0:T(8,128)S(1)}, f32[4,64,128]{2,1,0:T(8,128)S(1)}, u32[]{:S(2)}, u32[]{:S(2)}) collective-permute-start(f32[4,64,128]{2,1,0:T(8,128)S(1)} %fusion.83), channel_id=1, source_target_pairs={{0,8},{8,16},{16,24},{24,32},{32,40},{40,48},{48,56},{56,64},{64,7... | collective-permute-start | bytes 393224 | tf_op jit(solution)/shard_map/while/body/eval_jaxpr/ppermute | solution.py:15
  559.4 9.1 %collective-permute-start.1 = (f32[4,64,128]{2,1,0:T(8,128)S(1)}, f32[4,64,128]{2,1,0:T(8,128)S(1)}, u32[]{:S(2)}, u32[]{:S(2)}) collective-permute-start(f32[4,64,128]{2,1,0:T(8,128)S(1)} %fusion.83), channel_id=1, source_target_pairs={{0,8},{8,16},{16,24},{24,32},{32,40},{40,48},{48,56},{56,64},{64,7... | collective-permute-start | bytes 393224 | tf_op jit(solution)/shard_map/while/body/eval_jaxpr/ppermute | solution.py:15
  572.0 8.1 %collective-permute-start = (f32[4,64,128]{2,1,0:T(8,128)S(1)}, f32[4,64,128]{2,1,0:T(8,128)S(1)}, u32[]{:S(2)}, u32[]{:S(2)}) collective-permute-start(f32[4,64,128]{2,1,0:T(8,128)S(1)} %fusion.82), channel_id=1, source_target_pairs={{0,8},{8,16},{16,24},{24,32},{32,40},{40,48},{48,56},{56,64},{64,7... | collective-permute-start | bytes 393224 | tf_op jit(solution)/shard_map/while/body/eval_jaxpr/ppermute | solution.py:15
  572.3 9.1 %collective-permute-start.1 = (f32[4,64,128]{2,1,0:T(8,128)S(1)}, f32[4,64,128]{2,1,0:T(8,128)S(1)}, u32[]{:S(2)}, u32[]{:S(2)}) collective-permute-start(f32[4,64,128]{2,1,0:T(8,128)S(1)} %fusion.83), channel_id=1, source_target_pairs={{0,8},{8,16},{16,24},{24,32},{32,40},{40,48},{48,56},{56,64},{64,7... | collective-permute-start | bytes 393224 | tf_op jit(solution)/shard_map/while/body/eval_jaxpr/ppermute | solution.py:15
  584.9 8.1 %collective-permute-start = (f32[4,64,128]{2,1,0:T(8,128)S(1)}, f32[4,64,128]{2,1,0:T(8,128)S(1)}, u32[]{:S(2)}, u32[]{:S(2)}) collective-permute-start(f32[4,64,128]{2,1,0:T(8,128)S(1)} %fusion.82), channel_id=1, source_target_pairs={{0,8},{8,16},{16,24},{24,32},{32,40},{40,48},{48,56},{56,64},{64,7... | collective-permute-start | bytes 393224 | tf_op jit(solution)/shard_map/while/body/eval_jaxpr/ppermute | solution.py:15
  585.3 9.1 %collective-permute-start.1 = (f32[4,64,128]{2,1,0:T(8,128)S(1)}, f32[4,64,128]{2,1,0:T(8,128)S(1)}, u32[]{:S(2)}, u32[]{:S(2)}) collective-permute-start(f32[4,64,128]{2,1,0:T(8,128)S(1)} %fusion.83), channel_id=1, source_target_pairs={{0,8},{8,16},{16,24},{24,32},{32,40},{40,48},{48,56},{56,64},{64,7... | collective-permute-start | bytes 393224 | tf_op jit(solution)/shard_map/while/body/eval_jaxpr/ppermute | solution.py:15
  597.9 8.1 %collective-permute-start = (f32[4,64,128]{2,1,0:T(8,128)S(1)}, f32[4,64,128]{2,1,0:T(8,128)S(1)}, u32[]{:S(2)}, u32[]{:S(2)}) collective-permute-start(f32[4,64,128]{2,1,0:T(8,128)S(1)} %fusion.82), channel_id=1, source_target_pairs={{0,8},{8,16},{16,24},{24,32},{32,40},{40,48},{48,56},{56,64},{64,7... | collective-permute-start | bytes 393224 | tf_op jit(solution)/shard_map/while/body/eval_jaxpr/ppermute | solution.py:15
  598.3 9.1 %collective-permute-start.1 = (f32[4,64,128]{2,1,0:T(8,128)S(1)}, f32[4,64,128]{2,1,0:T(8,128)S(1)}, u32[]{:S(2)}, u32[]{:S(2)}) collective-permute-start(f32[4,64,128]{2,1,0:T(8,128)S(1)} %fusion.83), channel_id=1, source_target_pairs={{0,8},{8,16},{16,24},{24,32},{32,40},{40,48},{48,56},{56,64},{64,7... | collective-permute-start | bytes 393224 | tf_op jit(solution)/shard_map/while/body/eval_jaxpr/ppermute | solution.py:15
  610.9 8.1 %collective-permute-start = (f32[4,64,128]{2,1,0:T(8,128)S(1)}, f32[4,64,128]{2,1,0:T(8,128)S(1)}, u32[]{:S(2)}, u32[]{:S(2)}) collective-permute-start(f32[4,64,128]{2,1,0:T(8,128)S(1)} %fusion.82), channel_id=1, source_target_pairs={{0,8},{8,16},{16,24},{24,32},{32,40},{40,48},{48,56},{56,64},{64,7... | collective-permute-start | bytes 393224 | tf_op jit(solution)/shard_map/while/body/eval_jaxpr/ppermute | solution.py:15
  611.3 9.1 %collective-permute-start.1 = (f32[4,64,128]{2,1,0:T(8,128)S(1)}, f32[4,64,128]{2,1,0:T(8,128)S(1)}, u32[]{:S(2)}, u32[]{:S(2)}) collective-permute-start(f32[4,64,128]{2,1,0:T(8,128)S(1)} %fusion.83), channel_id=1, source_target_pairs={{0,8},{8,16},{16,24},{24,32},{32,40},{40,48},{48,56},{56,64},{64,7... | collective-permute-start | bytes 393224 | tf_op jit(solution)/shard_map/while/body/eval_jaxpr/ppermute | solution.py:15
  623.9 8.1 %collective-permute-start = (f32[4,64,128]{2,1,0:T(8,128)S(1)}, f32[4,64,128]{2,1,0:T(8,128)S(1)}, u32[]{:S(2)}, u32[]{:S(2)}) collective-permute-start(f32[4,64,128]{2,1,0:T(8,128)S(1)} %fusion.82), channel_id=1, source_target_pairs={{0,8},{8,16},{16,24},{24,32},{32,40},{40,48},{48,56},{56,64},{64,7... | collective-permute-start | bytes 393224 | tf_op jit(solution)/shard_map/while/body/eval_jaxpr/ppermute | solution.py:15
  624.2 9.1 %collective-permute-start.1 = (f32[4,64,128]{2,1,0:T(8,128)S(1)}, f32[4,64,128]{2,1,0:T(8,128)S(1)}, u32[]{:S(2)}, u32[]{:S(2)}) collective-permute-start(f32[4,64,128]{2,1,0:T(8,128)S(1)} %fusion.83), channel_id=1, source_target_pairs={{0,8},{8,16},{16,24},{24,32},{32,40},{40,48},{48,56},{56,64},{64,7... | collective-permute-start | bytes 393224 | tf_op jit(solution)/shard_map/while/body/eval_jaxpr/ppermute | solution.py:15
  634.1 10.8 %all-to-all-start.2 = ((bf16[4,64,128]{2,0,1:T(4,128)(2,1)}), bf16[4,64,128]{2,0,1:T(4,128)(2,1)S(1)}, u32[]{:S(2)}, u32[]{:S(2)}) async-start(bf16[4,64,128]{2,0,1:T(4,128)(2,1)} %copy.79), calls=%async_computation.2 | async-start | bytes 131072 | tf_op jit(solution)/shard_map/all_to_all | solution.py:146
  644.9 10.6 %all-to-all-start.1 = ((bf16[4,64,128]{2,0,1:T(4,128)(2,1)}), bf16[4,64,128]{2,0,1:T(4,128)(2,1)S(1)}, u32[]{:S(2)}, u32[]{:S(2)}) async-start(bf16[4,64,128]{2,0,1:T(4,128)(2,1)} %copy.80), calls=%async_computation.1 | async-start | bytes 131072 | tf_op jit(solution)/shard_map/all_to_all | solution.py:145
  655.5 11.6 %all-to-all-start = ((bf16[4,64,1024]{2,0,1:T(4,128)(2,1)}), bf16[4,64,1024]{2,0,1:T(4,128)(2,1)S(1)}, u32[]{:S(2)}, u32[]{:S(2)}) async-start(bf16[4,64,1024]{2,0,1:T(4,128)(2,1)} %reshape.190), calls=%async_computation | async-start | bytes 1048576 | tf_op jit(solution)/shard_map/all_to_all | solution.py:144
  (11 other events, 107.4 us)
Sparse Core Ops, SparseCore 0:
  10.8 82.0 all-gather.6
  95.8 76.5 all-gather.4
where the time goes:
time: 680 us; the launch traced here: 675 us
  waiting for transfers between devices  339 us (50%)
  matrix products  182 us (27%)
  blocking collectives  80.9 us (12%)
  starting transfers between devices  20.6 us (3%)
  other arithmetic  20 us (3%)
  local copies, waits for them, and re-layouts  16.3 us (2%)
  between operations  14.2 us (2%)
    ppermute x64, waiting for transfers between devices, passed_along(): lax.ppermute(array, axis, [(i, (i + by) % count) for i in range(count)])  245 us
    all_gather x1, waiting for transfers between devices, on_device(): lax.all_gather(key_vectors, 'ctx', axis=1, tiled=True)  76.3 us
    dot_general x36, matrix products, block_scores(): jnp.einsum('tkgd,skd->kgts', query_four_axes, key_three, preferred_elemen...  62.8 us
    dot_general x32, matrix products, block_grads(): jnp.einsum('tkgd,skd->kgts', grad_four, value_three, preferred_element_ty...  47.2 us
    all_gather x1, blocking collectives, on_device(): lax.all_gather(segments, 'ctx', axis=1, tiled=True)  44 us
    dot_general x32, matrix products, block_grads(): jnp.einsum('kgts,skd->tkgd', score_low, key_three, preferred_element_type...  41.9 us
    all_gather x1, blocking collectives, on_device(): lax.all_gather(positions, 'ctx', axis=1, tiled=True)  37 us
    reduce_sum x4, other arithmetic, stats_update(): new_sum = running_sum * rescale + jnp.sum(weights, axis=-1, keepdims=True)  14.7 us
  transfers between devices with their start and end apart: 69, of which 69 were waited for; matrix products, arithmetic and copies ran while one was open for 9% of the time, Pallas kernels for 0%

commit v1 on v0

--- a/solution.py
+++ b/solution.py
@@ -1,3 +1,4 @@
+import functools
 import math
 import jax
 import jax.numpy as jnp
@@ -8,6 +9,21 @@
 KEY_VALUE_HEADS = 8
 HEAD_SIZE = 128
 NEG_BIG = -1e30
+
+
+def surface_render(vec, along_axis, join_dim):
+    return jnp.concatenate(
+        lax.all_to_all(
+            jnp.stack([vec for _ in range(lax.axis_size(along_axis))]),
+            axis_name=along_axis,
+            split_axis=0,
+            concat_axis=0,
+        ),
+        axis=join_dim,
+    )
+
+
+number_cycles = functools.partial(surface_render, along_axis="ctx", join_dim=1)
 
 
 def passed_along(array, axis, by):
@@ -94,7 +110,7 @@
     stats_many = jax.vmap(stats_update)
     grads_many = jax.vmap(block_grads)
     gathered = (
-        lax.all_gather(key_vectors, "ctx", axis=1, tiled=True),
+        number_cycles(key_vectors),
         lax.all_gather(value_vectors, "ctx", axis=1, tiled=True),
         lax.all_gather(positions, "ctx", axis=1, tiled=True),
         lax.all_gather(segments, "ctx", axis=1, tiled=True),

time: 680 us -> 655 us (0.963)
  waiting for transfers between devices: 339 us -> 260 us
  blocking collectives: 80.9 us -> 121 us
  starting transfers between devices: 20.6 us -> 32.3 us
    all_gather x1 -> x0, waiting for transfers between devices: 76.3 us -> none  [on_device(): lax.all_gather(key_vectors, 'ctx', axis=1, tiled=True)]
    all_gather x1, blocking collectives: 37 us -> 84.3 us  [on_device(): lax.all_gather(positions, 'ctx', axis=1, tiled=True)]
    all_to_all x0 -> x1, starting transfers between devices: none -> 10.7 us  [surface_render(): lax.all_to_all(jnp.stack([vec for _ in range(lax.axis_size(along_axis))])...]
    all_gather x1, blocking collectives: 44 us -> 36.9 us  [on_device(): lax.all_gather(segments, 'ctx', axis=1, tiled=True)]
  transfers between devices with their start and end apart: 69 -> 69, of which waited for: 69 -> 67; matrix products, arithmetic and copies ran while one was open for 9% -> 9% of each run, Pallas kernels for 0% -> 0%
where the time goes in v1:
time: 655 us; the launch traced here: 649 us
  waiting for transfers between devices  260 us (40%)
  matrix products  182 us (28%)
  blocking collectives  121 us (18%)
  starting transfers between devices  32.3 us (5%)
  other arithmetic  20 us (3%)
  local copies, waits for them, and re-layouts  17 us (3%)
  between operations  14.2 us (2%)
    ppermute x64, waiting for transfers between devices, passed_along(): lax.ppermute(array, axis, [(i, (i + by) % count) for i in range(count)])  244 us
    all_gather x1, blocking collectives, on_device(): lax.all_gather(positions, 'ctx', axis=1, tiled=True)  84.3 us
    dot_general x36, matrix products, block_scores(): jnp.einsum('tkgd,skd->kgts', query_four_axes, key_three, preferred_elemen...  62.9 us
    dot_general x32, matrix products, block_grads(): jnp.einsum('tkgd,skd->kgts', grad_four, value_three, preferred_element_ty...  47.2 us
    dot_general x32, matrix products, block_grads(): jnp.einsum('kgts,skd->tkgd', score_low, key_three, preferred_element_type...  41.9 us
    all_gather x1, blocking collectives, on_device(): lax.all_gather(segments, 'ctx', axis=1, tiled=True)  36.9 us
    reduce_sum x4, other arithmetic, stats_update(): new_sum = running_sum * rescale + jnp.sum(weights, axis=-1, keepdims=True)  14.7 us
  transfers between devices with their start and end apart: 69, of which 67 were waited for; matrix products, arithmetic and copies ran while one was open for 9% of the time, Pallas kernels for 0%

profile of v1, /device:TPU:2, one launch (start us, length us, event | category | flops | bytes accessed | tf_op | source)
XLA Modules:
  0.0 649.3 jit_solution(2152304552630235395)
XLA Ops:
  7.9 2.8 stack.2
  10.7 10.7 %all-to-all-start = ((bf16[32,4,64,128]{3,2,1,0:T(8,128)(2,1)}), bf16[32,4,64,128]{3,2,1,0:T(8,128)(2,1)}, u32[]{:S(2)}, u32[]{:S(2)}) async-start(bf16[32,4,64,128]{3,2,1,0:T(8,128)(2,1)} %stack.2), calls=%async_computation | async-start | bytes 4194304 | tf_op jit(solution)/shard_map/all_to_all | solution.py:16
  21.9 84.3 %all-gather.1 = s32[32,64,4]{1,2,0:T(4,128)S(1)} all-gather(s32[1,64,4]{1,2,0:T(4,128)S(1)} %bitcast.263), channel_id=1, replica_groups=mesh['ctx'=32,'head'=8] {'ctx'}, dimensions={0}, use_global_device_ids=true | all-gather | bytes 33792 | tf_op jit(solution)/shard_map/all_gather | solution.py:115
  106.3 36.9 %all-gather = s32[32,64,4]{1,2,0:T(4,128)S(1)} all-gather(s32[1,64,4]{1,2,0:T(4,128)S(1)} %bitcast.262), channel_id=1, replica_groups=mesh['ctx'=32,'head'=8] {'ctx'}, dimensions={0}, use_global_device_ids=true | all-gather | bytes 33792 | tf_op jit(solution)/shard_map/all_gather | solution.py:116
  143.3 3.2 copy.82
  146.5 3.2 copy.45
  149.7 42.5 %while.35 = (s32[]{:T(128)}, f32[4,1,8,64,1]{3,2,0,4,1:T(8,128)S(1)}, f32[4,1,8,64,1]{3,2,0,4,1:T(8,128)S(1)}, f32[4,1,8,64,1]{3,2,0,4,1:T(8,128)S(1)}, s32[4,64...) while((s32[]{:T(128)}, ...), condition=%wide.region_4.5_spmd.clone, body=%wide.region_0.4_spmd.clone.sunk | while | flops 551958528 | bytes 32181424 | solution.py:133
  149.8 3.8 fusion.66
  153.6 3.7 fusion.68
  157.3 2.9 fusion.67
  160.5 3.8 fusion.66
  164.3 3.7 fusion.68
  168.0 2.9 fusion.67
  171.1 3.8 fusion.66
  174.9 3.7 fusion.68
  178.6 2.9 fusion.67
  181.7 3.8 fusion.66
  185.5 3.7 fusion.68
  189.2 2.9 fusion.67
  192.2 415.3 %while.36 = (s32[]{:T(128)}, f32[4,64,1,8,128]{4,1,3,0,2:T(8,128)S(1)}, f32[4,64,128]{2,1,0:T(8,128)S(1)}, f32[4,64,128]{2,1,0:T(8,128)S(1)}, s32[]{:T(128)}, /*...) while((s32[]{:T(128)}, ...), condition=%wide.region_6.7_spmd.clone, body=%wide.region_5.6_spmd.clone.sunk | while | flops 169754640 | bytes 8380878 | solution.py:153
  196.4 1.5 collective-permute-start.1
  199.3 4.6 collective-permute-done
  205.5 1.5 fusion.79
  210.5 6.3 collective-permute-done
  218.4 1.5 fusion.79
  223.5 6.3 collective-permute-done
  231.4 1.5 fusion.79
  236.5 6.3 collective-permute-done
  249.5 6.3 collective-permute-done
  262.4 6.3 collective-permute-done
  275.4 6.3 collective-permute-done
  288.4 6.3 collective-permute-done
  296.3 1.5 fusion.79
  301.4 6.3 collective-permute-done
  309.3 1.5 fusion.79
  314.3 6.3 collective-permute-done
  327.3 6.3 collective-permute-done
  340.3 6.3 collective-permute-done
  353.3 6.3 collective-permute-done
  366.3 6.3 collective-permute-done
  379.2 6.3 collective-permute-done
  392.2 6.3 collective-permute-done
  405.2 6.3 collective-permute-done
  418.2 6.3 collective-permute-done
  431.1 6.3 collective-permute-done
  444.1 6.3 collective-permute-done
  457.1 6.3 collective-permute-done
  470.1 6.3 collective-permute-done
  483.0 6.3 collective-permute-done
  496.0 6.3 collective-permute-done
  509.0 6.3 collective-permute-done
  522.0 6.3 collective-permute-done
  535.0 6.3 collective-permute-done
  547.9 6.3 collective-permute-done
  560.9 6.3 collective-permute-done
  573.9 6.3 collective-permute-done
  586.9 6.3 collective-permute-done
  599.8 6.3 collective-permute-done
  608.3 6.0 all-to-all-start.3
  614.9 4.3 all-to-all-done.3
  619.3 4.5 all-to-all-start.2
  625.2 4.7 all-to-all-done.2
  629.9 4.0 all-to-all-start.1
  635.2 6.3 all-to-all-done.1
  (377 shorter events, 212.1 us)
Async XLA Ops:
  7.2 136.1 %all-gather.4.cloned.1.call-start = ((), (), s32[]{:S(2)}) async-start(), calls=%async_computation.4 | async-start | bytes 2162688 | tf_op jit(solution)/shard_map/all_gather | solution.py:114
  10.7 135.8 %all-to-all-start = ((bf16[32,4,64,128]{3,2,1,0:T(8,128)(2,1)}), bf16[32,4,64,128]{3,2,1,0:T(8,128)(2,1)}, u32[]{:S(2)}, u32[]{:S(2)}) async-start(bf16[32,4,64,128]{3,2,1,0:T(8,128)(2,1)} %stack.2), calls=%async_computation | async-start | bytes 4194304 | tf_op jit(solution)/shard_map/all_to_all | solution.py:16
  195.8 8.1 %collective-permute-start = (f32[4,64,128]{2,1,0:T(8,128)S(1)}, f32[4,64,128]{2,1,0:T(8,128)S(1)}, u32[]{:S(2)}, u32[]{:S(2)}) collective-permute-start(f32[4,64,128]{2,1,0:T(8,128)S(1)} %fusion.82), channel_id=1, source_target_pairs={{0,8},{8,16},{16,24},{24,32},{32,40},{40,48},{48,56},{56,64},{64,7... | collective-permute-start | bytes 393224 | tf_op jit(solution)/shard_map/while/body/eval_jaxpr/ppermute | solution.py:31
  196.4 8.8 %collective-permute-start.1 = (f32[4,64,128]{2,1,0:T(8,128)S(1)}, f32[4,64,128]{2,1,0:T(8,128)S(1)}, u32[]{:S(2)}, u32[]{:S(2)}) collective-permute-start(f32[4,64,128]{2,1,0:T(8,128)S(1)} %fusion.83), channel_id=1, source_target_pairs={{0,8},{8,16},{16,24},{24,32},{32,40},{40,48},{48,56},{56,64},{64,7... | collective-permute-start | bytes 393224 | tf_op jit(solution)/shard_map/while/body/eval_jaxpr/ppermute | solution.py:31
  208.7 8.1 %collective-permute-start = (f32[4,64,128]{2,1,0:T(8,128)S(1)}, f32[4,64,128]{2,1,0:T(8,128)S(1)}, u32[]{:S(2)}, u32[]{:S(2)}) collective-permute-start(f32[4,64,128]{2,1,0:T(8,128)S(1)} %fusion.82), channel_id=1, source_target_pairs={{0,8},{8,16},{16,24},{24,32},{32,40},{40,48},{48,56},{56,64},{64,7... | collective-permute-start | bytes 393224 | tf_op jit(solution)/shard_map/while/body/eval_jaxpr/ppermute | solution.py:31
  209.1 9.1 %collective-permute-start.1 = (f32[4,64,128]{2,1,0:T(8,128)S(1)}, f32[4,64,128]{2,1,0:T(8,128)S(1)}, u32[]{:S(2)}, u32[]{:S(2)}) collective-permute-start(f32[4,64,128]{2,1,0:T(8,128)S(1)} %fusion.83), channel_id=1, source_target_pairs={{0,8},{8,16},{16,24},{24,32},{32,40},{40,48},{48,56},{56,64},{64,7... | collective-permute-start | bytes 393224 | tf_op jit(solution)/shard_map/while/body/eval_jaxpr/ppermute | solution.py:31
  221.7 8.1 %collective-permute-start = (f32[4,64,128]{2,1,0:T(8,128)S(1)}, f32[4,64,128]{2,1,0:T(8,128)S(1)}, u32[]{:S(2)}, u32[]{:S(2)}) collective-permute-start(f32[4,64,128]{2,1,0:T(8,128)S(1)} %fusion.82), channel_id=1, source_target_pairs={{0,8},{8,16},{16,24},{24,32},{32,40},{40,48},{48,56},{56,64},{64,7... | collective-permute-start | bytes 393224 | tf_op jit(solution)/shard_map/while/body/eval_jaxpr/ppermute | solution.py:31
  222.1 9.1 %collective-permute-start.1 = (f32[4,64,128]{2,1,0:T(8,128)S(1)}, f32[4,64,128]{2,1,0:T(8,128)S(1)}, u32[]{:S(2)}, u32[]{:S(2)}) collective-permute-start(f32[4,64,128]{2,1,0:T(8,128)S(1)} %fusion.83), channel_id=1, source_target_pairs={{0,8},{8,16},{16,24},{24,32},{32,40},{40,48},{48,56},{56,64},{64,7... | collective-permute-start | bytes 393224 | tf_op jit(solution)/shard_map/while/body/eval_jaxpr/ppermute | solution.py:31
  234.7 8.1 %collective-permute-start = (f32[4,64,128]{2,1,0:T(8,128)S(1)}, f32[4,64,128]{2,1,0:T(8,128)S(1)}, u32[]{:S(2)}, u32[]{:S(2)}) collective-permute-start(f32[4,64,128]{2,1,0:T(8,128)S(1)} %fusion.82), channel_id=1, source_target_pairs={{0,8},{8,16},{16,24},{24,32},{32,40},{40,48},{48,56},{56,64},{64,7... | collective-permute-start | bytes 393224 | tf_op jit(solution)/shard_map/while/body/eval_jaxpr/ppermute | solution.py:31
  235.1 9.1 %collective-permute-start.1 = (f32[4,64,128]{2,1,0:T(8,128)S(1)}, f32[4,64,128]{2,1,0:T(8,128)S(1)}, u32[]{:S(2)}, u32[]{:S(2)}) collective-permute-start(f32[4,64,128]{2,1,0:T(8,128)S(1)} %fusion.83), channel_id=1, source_target_pairs={{0,8},{8,16},{16,24},{24,32},{32,40},{40,48},{48,56},{56,64},{64,7... | collective-permute-start | bytes 393224 | tf_op jit(solution)/shard_map/while/body/eval_jaxpr/ppermute | solution.py:31
  247.7 8.1 %collective-permute-start = (f32[4,64,128]{2,1,0:T(8,128)S(1)}, f32[4,64,128]{2,1,0:T(8,128)S(1)}, u32[]{:S(2)}, u32[]{:S(2)}) collective-permute-start(f32[4,64,128]{2,1,0:T(8,128)S(1)} %fusion.82), channel_id=1, source_target_pairs={{0,8},{8,16},{16,24},{24,32},{32,40},{40,48},{48,56},{56,64},{64,7... | collective-permute-start | bytes 393224 | tf_op jit(solution)/shard_map/while/body/eval_jaxpr/ppermute | solution.py:31
  248.0 9.1 %collective-permute-start.1 = (f32[4,64,128]{2,1,0:T(8,128)S(1)}, f32[4,64,128]{2,1,0:T(8,128)S(1)}, u32[]{:S(2)}, u32[]{:S(2)}) collective-permute-start(f32[4,64,128]{2,1,0:T(8,128)S(1)} %fusion.83), channel_id=1, source_target_pairs={{0,8},{8,16},{16,24},{24,32},{32,40},{40,48},{48,56},{56,64},{64,7... | collective-permute-start | bytes 393224 | tf_op jit(solution)/shard_map/while/body/eval_jaxpr/ppermute | solution.py:31
  260.6 8.1 %collective-permute-start = (f32[4,64,128]{2,1,0:T(8,128)S(1)}, f32[4,64,128]{2,1,0:T(8,128)S(1)}, u32[]{:S(2)}, u32[]{:S(2)}) collective-permute-start(f32[4,64,128]{2,1,0:T(8,128)S(1)} %fusion.82), channel_id=1, source_target_pairs={{0,8},{8,16},{16,24},{24,32},{32,40},{40,48},{48,56},{56,64},{64,7... | collective-permute-start | bytes 393224 | tf_op jit(solution)/shard_map/while/body/eval_jaxpr/ppermute | solution.py:31
  261.0 9.1 %collective-permute-start.1 = (f32[4,64,128]{2,1,0:T(8,128)S(1)}, f32[4,64,128]{2,1,0:T(8,128)S(1)}, u32[]{:S(2)}, u32[]{:S(2)}) collective-permute-start(f32[4,64,128]{2,1,0:T(8,128)S(1)} %fusion.83), channel_id=1, source_target_pairs={{0,8},{8,16},{16,24},{24,32},{32,40},{40,48},{48,56},{56,64},{64,7... | collective-permute-start | bytes 393224 | tf_op jit(solution)/shard_map/while/body/eval_jaxpr/ppermute | solution.py:31
  273.6 8.1 %collective-permute-start = (f32[4,64,128]{2,1,0:T(8,128)S(1)}, f32[4,64,128]{2,1,0:T(8,128)S(1)}, u32[]{:S(2)}, u32[]{:S(2)}) collective-permute-start(f32[4,64,128]{2,1,0:T(8,128)S(1)} %fusion.82), channel_id=1, source_target_pairs={{0,8},{8,16},{16,24},{24,32},{32,40},{40,48},{48,56},{56,64},{64,7... | collective-permute-start | bytes 393224 | tf_op jit(solution)/shard_map/while/body/eval_jaxpr/ppermute | solution.py:31
  274.0 9.1 %collective-permute-start.1 = (f32[4,64,128]{2,1,0:T(8,128)S(1)}, f32[4,64,128]{2,1,0:T(8,128)S(1)}, u32[]{:S(2)}, u32[]{:S(2)}) collective-permute-start(f32[4,64,128]{2,1,0:T(8,128)S(1)} %fusion.83), channel_id=1, source_target_pairs={{0,8},{8,16},{16,24},{24,32},{32,40},{40,48},{48,56},{56,64},{64,7... | collective-permute-start | bytes 393224 | tf_op jit(solution)/shard_map/while/body/eval_jaxpr/ppermute | solution.py:31
  286.6 8.1 %collective-permute-start = (f32[4,64,128]{2,1,0:T(8,128)S(1)}, f32[4,64,128]{2,1,0:T(8,128)S(1)}, u32[]{:S(2)}, u32[]{:S(2)}) collective-permute-start(f32[4,64,128]{2,1,0:T(8,128)S(1)} %fusion.82), channel_id=1, source_target_pairs={{0,8},{8,16},{16,24},{24,32},{32,40},{40,48},{48,56},{56,64},{64,7... | collective-permute-start | bytes 393224 | tf_op jit(solution)/shard_map/while/body/eval_jaxpr/ppermute | solution.py:31
  287.0 9.1 %collective-permute-start.1 = (f32[4,64,128]{2,1,0:T(8,128)S(1)}, f32[4,64,128]{2,1,0:T(8,128)S(1)}, u32[]{:S(2)}, u32[]{:S(2)}) collective-permute-start(f32[4,64,128]{2,1,0:T(8,128)S(1)} %fusion.83), channel_id=1, source_target_pairs={{0,8},{8,16},{16,24},{24,32},{32,40},{40,48},{48,56},{56,64},{64,7... | collective-permute-start | bytes 393224 | tf_op jit(solution)/shard_map/while/body/eval_jaxpr/ppermute | solution.py:31
  299.6 8.1 %collective-permute-start = (f32[4,64,128]{2,1,0:T(8,128)S(1)}, f32[4,64,128]{2,1,0:T(8,128)S(1)}, u32[]{:S(2)}, u32[]{:S(2)}) collective-permute-start(f32[4,64,128]{2,1,0:T(8,128)S(1)} %fusion.82), channel_id=1, source_target_pairs={{0,8},{8,16},{16,24},{24,32},{32,40},{40,48},{48,56},{56,64},{64,7... | collective-permute-start | bytes 393224 | tf_op jit(solution)/shard_map/while/body/eval_jaxpr/ppermute | solution.py:31
  300.0 9.1 %collective-permute-start.1 = (f32[4,64,128]{2,1,0:T(8,128)S(1)}, f32[4,64,128]{2,1,0:T(8,128)S(1)}, u32[]{:S(2)}, u32[]{:S(2)}) collective-permute-start(f32[4,64,128]{2,1,0:T(8,128)S(1)} %fusion.83), channel_id=1, source_target_pairs={{0,8},{8,16},{16,24},{24,32},{32,40},{40,48},{48,56},{56,64},{64,7... | collective-permute-start | bytes 393224 | tf_op jit(solution)/shard_map/while/body/eval_jaxpr/ppermute | solution.py:31
  312.6 8.1 %collective-permute-start = (f32[4,64,128]{2,1,0:T(8,128)S(1)}, f32[4,64,128]{2,1,0:T(8,128)S(1)}, u32[]{:S(2)}, u32[]{:S(2)}) collective-permute-start(f32[4,64,128]{2,1,0:T(8,128)S(1)} %fusion.82), channel_id=1, source_target_pairs={{0,8},{8,16},{16,24},{24,32},{32,40},{40,48},{48,56},{56,64},{64,7... | collective-permute-start | bytes 393224 | tf_op jit(solution)/shard_map/while/body/eval_jaxpr/ppermute | solution.py:31
  312.9 9.1 %collective-permute-start.1 = (f32[4,64,128]{2,1,0:T(8,128)S(1)}, f32[4,64,128]{2,1,0:T(8,128)S(1)}, u32[]{:S(2)}, u32[]{:S(2)}) collective-permute-start(f32[4,64,128]{2,1,0:T(8,128)S(1)} %fusion.83), channel_id=1, source_target_pairs={{0,8},{8,16},{16,24},{24,32},{32,40},{40,48},{48,56},{56,64},{64,7... | collective-permute-start | bytes 393224 | tf_op jit(solution)/shard_map/while/body/eval_jaxpr/ppermute | solution.py:31
  325.5 8.1 %collective-permute-start = (f32[4,64,128]{2,1,0:T(8,128)S(1)}, f32[4,64,128]{2,1,0:T(8,128)S(1)}, u32[]{:S(2)}, u32[]{:S(2)}) collective-permute-start(f32[4,64,128]{2,1,0:T(8,128)S(1)} %fusion.82), channel_id=1, source_target_pairs={{0,8},{8,16},{16,24},{24,32},{32,40},{40,48},{48,56},{56,64},{64,7... | collective-permute-start | bytes 393224 | tf_op jit(solution)/shard_map/while/body/eval_jaxpr/ppermute | solution.py:31
  325.9 9.1 %collective-permute-start.1 = (f32[4,64,128]{2,1,0:T(8,128)S(1)}, f32[4,64,128]{2,1,0:T(8,128)S(1)}, u32[]{:S(2)}, u32[]{:S(2)}) collective-permute-start(f32[4,64,128]{2,1,0:T(8,128)S(1)} %fusion.83), channel_id=1, source_target_pairs={{0,8},{8,16},{16,24},{24,32},{32,40},{40,48},{48,56},{56,64},{64,7... | collective-permute-start | bytes 393224 | tf_op jit(solution)/shard_map/while/body/eval_jaxpr/ppermute | solution.py:31
  338.5 8.1 %collective-permute-start = (f32[4,64,128]{2,1,0:T(8,128)S(1)}, f32[4,64,128]{2,1,0:T(8,128)S(1)}, u32[]{:S(2)}, u32[]{:S(2)}) collective-permute-start(f32[4,64,128]{2,1,0:T(8,128)S(1)} %fusion.82), channel_id=1, source_target_pairs={{0,8},{8,16},{16,24},{24,32},{32,40},{40,48},{48,56},{56,64},{64,7... | collective-permute-start | bytes 393224 | tf_op jit(solution)/shard_map/while/body/eval_jaxpr/ppermute | solution.py:31
  338.9 9.1 %collective-permute-start.1 = (f32[4,64,128]{2,1,0:T(8,128)S(1)}, f32[4,64,128]{2,1,0:T(8,128)S(1)}, u32[]{:S(2)}, u32[]{:S(2)}) collective-permute-start(f32[4,64,128]{2,1,0:T(8,128)S(1)} %fusion.83), channel_id=1, source_target_pairs={{0,8},{8,16},{16,24},{24,32},{32,40},{40,48},{48,56},{56,64},{64,7... | collective-permute-start | bytes 393224 | tf_op jit(solution)/shard_map/while/body/eval_jaxpr/ppermute | solution.py:31
  351.5 8.1 %collective-permute-start = (f32[4,64,128]{2,1,0:T(8,128)S(1)}, f32[4,64,128]{2,1,0:T(8,128)S(1)}, u32[]{:S(2)}, u32[]{:S(2)}) collective-permute-start(f32[4,64,128]{2,1,0:T(8,128)S(1)} %fusion.82), channel_id=1, source_target_pairs={{0,8},{8,16},{16,24},{24,32},{32,40},{40,48},{48,56},{56,64},{64,7... | collective-permute-start | bytes 393224 | tf_op jit(solution)/shard_map/while/body/eval_jaxpr/ppermute | solution.py:31
  351.9 9.1 %collective-permute-start.1 = (f32[4,64,128]{2,1,0:T(8,128)S(1)}, f32[4,64,128]{2,1,0:T(8,128)S(1)}, u32[]{:S(2)}, u32[]{:S(2)}) collective-permute-start(f32[4,64,128]{2,1,0:T(8,128)S(1)} %fusion.83), channel_id=1, source_target_pairs={{0,8},{8,16},{16,24},{24,32},{32,40},{40,48},{48,56},{56,64},{64,7... | collective-permute-start | bytes 393224 | tf_op jit(solution)/shard_map/while/body/eval_jaxpr/ppermute | solution.py:31
  364.5 8.1 %collective-permute-start = (f32[4,64,128]{2,1,0:T(8,128)S(1)}, f32[4,64,128]{2,1,0:T(8,128)S(1)}, u32[]{:S(2)}, u32[]{:S(2)}) collective-permute-start(f32[4,64,128]{2,1,0:T(8,128)S(1)} %fusion.82), channel_id=1, source_target_pairs={{0,8},{8,16},{16,24},{24,32},{32,40},{40,48},{48,56},{56,64},{64,7... | collective-permute-start | bytes 393224 | tf_op jit(solution)/shard_map/while/body/eval_jaxpr/ppermute | solution.py:31
  364.8 9.1 %collective-permute-start.1 = (f32[4,64,128]{2,1,0:T(8,128)S(1)}, f32[4,64,128]{2,1,0:T(8,128)S(1)}, u32[]{:S(2)}, u32[]{:S(2)}) collective-permute-start(f32[4,64,128]{2,1,0:T(8,128)S(1)} %fusion.83), channel_id=1, source_target_pairs={{0,8},{8,16},{16,24},{24,32},{32,40},{40,48},{48,56},{56,64},{64,7... | collective-permute-start | bytes 393224 | tf_op jit(solution)/shard_map/while/body/eval_jaxpr/ppermute | solution.py:31
  377.4 8.1 %collective-permute-start = (f32[4,64,128]{2,1,0:T(8,128)S(1)}, f32[4,64,128]{2,1,0:T(8,128)S(1)}, u32[]{:S(2)}, u32[]{:S(2)}) collective-permute-start(f32[4,64,128]{2,1,0:T(8,128)S(1)} %fusion.82), channel_id=1, source_target_pairs={{0,8},{8,16},{16,24},{24,32},{32,40},{40,48},{48,56},{56,64},{64,7... | collective-permute-start | bytes 393224 | tf_op jit(solution)/shard_map/while/body/eval_jaxpr/ppermute | solution.py:31
  377.8 9.1 %collective-permute-start.1 = (f32[4,64,128]{2,1,0:T(8,128)S(1)}, f32[4,64,128]{2,1,0:T(8,128)S(1)}, u32[]{:S(2)}, u32[]{:S(2)}) collective-permute-start(f32[4,64,128]{2,1,0:T(8,128)S(1)} %fusion.83), channel_id=1, source_target_pairs={{0,8},{8,16},{16,24},{24,32},{32,40},{40,48},{48,56},{56,64},{64,7... | collective-permute-start | bytes 393224 | tf_op jit(solution)/shard_map/while/body/eval_jaxpr/ppermute | solution.py:31
  390.4 8.1 %collective-permute-start = (f32[4,64,128]{2,1,0:T(8,128)S(1)}, f32[4,64,128]{2,1,0:T(8,128)S(1)}, u32[]{:S(2)}, u32[]{:S(2)}) collective-permute-start(f32[4,64,128]{2,1,0:T(8,128)S(1)} %fusion.82), channel_id=1, source_target_pairs={{0,8},{8,16},{16,24},{24,32},{32,40},{40,48},{48,56},{56,64},{64,7... | collective-permute-start | bytes 393224 | tf_op jit(solution)/shard_map/while/body/eval_jaxpr/ppermute | solution.py:31
  390.8 9.1 %collective-permute-start.1 = (f32[4,64,128]{2,1,0:T(8,128)S(1)}, f32[4,64,128]{2,1,0:T(8,128)S(1)}, u32[]{:S(2)}, u32[]{:S(2)}) collective-permute-start(f32[4,64,128]{2,1,0:T(8,128)S(1)} %fusion.83), channel_id=1, source_target_pairs={{0,8},{8,16},{16,24},{24,32},{32,40},{40,48},{48,56},{56,64},{64,7... | collective-permute-start | bytes 393224 | tf_op jit(solution)/shard_map/while/body/eval_jaxpr/ppermute | solution.py:31
  403.4 8.1 %collective-permute-start = (f32[4,64,128]{2,1,0:T(8,128)S(1)}, f32[4,64,128]{2,1,0:T(8,128)S(1)}, u32[]{:S(2)}, u32[]{:S(2)}) collective-permute-start(f32[4,64,128]{2,1,0:T(8,128)S(1)} %fusion.82), channel_id=1, source_target_pairs={{0,8},{8,16},{16,24},{24,32},{32,40},{40,48},{48,56},{56,64},{64,7... | collective-permute-start | bytes 393224 | tf_op jit(solution)/shard_map/while/body/eval_jaxpr/ppermute | solution.py:31
  403.8 9.1 %collective-permute-start.1 = (f32[4,64,128]{2,1,0:T(8,128)S(1)}, f32[4,64,128]{2,1,0:T(8,128)S(1)}, u32[]{:S(2)}, u32[]{:S(2)}) collective-permute-start(f32[4,64,128]{2,1,0:T(8,128)S(1)} %fusion.83), channel_id=1, source_target_pairs={{0,8},{8,16},{16,24},{24,32},{32,40},{40,48},{48,56},{56,64},{64,7... | collective-permute-start | bytes 393224 | tf_op jit(solution)/shard_map/while/body/eval_jaxpr/ppermute | solution.py:31
  416.4 8.1 %collective-permute-start = (f32[4,64,128]{2,1,0:T(8,128)S(1)}, f32[4,64,128]{2,1,0:T(8,128)S(1)}, u32[]{:S(2)}, u32[]{:S(2)}) collective-permute-start(f32[4,64,128]{2,1,0:T(8,128)S(1)} %fusion.82), channel_id=1, source_target_pairs={{0,8},{8,16},{16,24},{24,32},{32,40},{40,48},{48,56},{56,64},{64,7... | collective-permute-start | bytes 393224 | tf_op jit(solution)/shard_map/while/body/eval_jaxpr/ppermute | solution.py:31
  416.7 9.1 %collective-permute-start.1 = (f32[4,64,128]{2,1,0:T(8,128)S(1)}, f32[4,64,128]{2,1,0:T(8,128)S(1)}, u32[]{:S(2)}, u32[]{:S(2)}) collective-permute-start(f32[4,64,128]{2,1,0:T(8,128)S(1)} %fusion.83), channel_id=1, source_target_pairs={{0,8},{8,16},{16,24},{24,32},{32,40},{40,48},{48,56},{56,64},{64,7... | collective-permute-start | bytes 393224 | tf_op jit(solution)/shard_map/while/body/eval_jaxpr/ppermute | solution.py:31
  429.3 8.1 %collective-permute-start = (f32[4,64,128]{2,1,0:T(8,128)S(1)}, f32[4,64,128]{2,1,0:T(8,128)S(1)}, u32[]{:S(2)}, u32[]{:S(2)}) collective-permute-start(f32[4,64,128]{2,1,0:T(8,128)S(1)} %fusion.82), channel_id=1, source_target_pairs={{0,8},{8,16},{16,24},{24,32},{32,40},{40,48},{48,56},{56,64},{64,7... | collective-permute-start | bytes 393224 | tf_op jit(solution)/shard_map/while/body/eval_jaxpr/ppermute | solution.py:31
  429.7 9.1 %collective-permute-start.1 = (f32[4,64,128]{2,1,0:T(8,128)S(1)}, f32[4,64,128]{2,1,0:T(8,128)S(1)}, u32[]{:S(2)}, u32[]{:S(2)}) collective-permute-start(f32[4,64,128]{2,1,0:T(8,128)S(1)} %fusion.83), channel_id=1, source_target_pairs={{0,8},{8,16},{16,24},{24,32},{32,40},{40,48},{48,56},{56,64},{64,7... | collective-permute-start | bytes 393224 | tf_op jit(solution)/shard_map/while/body/eval_jaxpr/ppermute | solution.py:31
  442.3 8.1 %collective-permute-start = (f32[4,64,128]{2,1,0:T(8,128)S(1)}, f32[4,64,128]{2,1,0:T(8,128)S(1)}, u32[]{:S(2)}, u32[]{:S(2)}) collective-permute-start(f32[4,64,128]{2,1,0:T(8,128)S(1)} %fusion.82), channel_id=1, source_target_pairs={{0,8},{8,16},{16,24},{24,32},{32,40},{40,48},{48,56},{56,64},{64,7... | collective-permute-start | bytes 393224 | tf_op jit(solution)/shard_map/while/body/eval_jaxpr/ppermute | solution.py:31
  442.7 9.1 %collective-permute-start.1 = (f32[4,64,128]{2,1,0:T(8,128)S(1)}, f32[4,64,128]{2,1,0:T(8,128)S(1)}, u32[]{:S(2)}, u32[]{:S(2)}) collective-permute-start(f32[4,64,128]{2,1,0:T(8,128)S(1)} %fusion.83), channel_id=1, source_target_pairs={{0,8},{8,16},{16,24},{24,32},{32,40},{40,48},{48,56},{56,64},{64,7... | collective-permute-start | bytes 393224 | tf_op jit(solution)/shard_map/while/body/eval_jaxpr/ppermute | solution.py:31
  455.3 8.1 %collective-permute-start = (f32[4,64,128]{2,1,0:T(8,128)S(1)}, f32[4,64,128]{2,1,0:T(8,128)S(1)}, u32[]{:S(2)}, u32[]{:S(2)}) collective-permute-start(f32[4,64,128]{2,1,0:T(8,128)S(1)} %fusion.82), channel_id=1, source_target_pairs={{0,8},{8,16},{16,24},{24,32},{32,40},{40,48},{48,56},{56,64},{64,7... | collective-permute-start | bytes 393224 | tf_op jit(solution)/shard_map/while/body/eval_jaxpr/ppermute | solution.py:31
  455.7 9.1 %collective-permute-start.1 = (f32[4,64,128]{2,1,0:T(8,128)S(1)}, f32[4,64,128]{2,1,0:T(8,128)S(1)}, u32[]{:S(2)}, u32[]{:S(2)}) collective-permute-start(f32[4,64,128]{2,1,0:T(8,128)S(1)} %fusion.83), channel_id=1, source_target_pairs={{0,8},{8,16},{16,24},{24,32},{32,40},{40,48},{48,56},{56,64},{64,7... | collective-permute-start | bytes 393224 | tf_op jit(solution)/shard_map/while/body/eval_jaxpr/ppermute | solution.py:31
  468.3 8.1 %collective-permute-start = (f32[4,64,128]{2,1,0:T(8,128)S(1)}, f32[4,64,128]{2,1,0:T(8,128)S(1)}, u32[]{:S(2)}, u32[]{:S(2)}) collective-permute-start(f32[4,64,128]{2,1,0:T(8,128)S(1)} %fusion.82), channel_id=1, source_target_pairs={{0,8},{8,16},{16,24},{24,32},{32,40},{40,48},{48,56},{56,64},{64,7... | collective-permute-start | bytes 393224 | tf_op jit(solution)/shard_map/while/body/eval_jaxpr/ppermute | solution.py:31
  468.7 9.1 %collective-permute-start.1 = (f32[4,64,128]{2,1,0:T(8,128)S(1)}, f32[4,64,128]{2,1,0:T(8,128)S(1)}, u32[]{:S(2)}, u32[]{:S(2)}) collective-permute-start(f32[4,64,128]{2,1,0:T(8,128)S(1)} %fusion.83), channel_id=1, source_target_pairs={{0,8},{8,16},{16,24},{24,32},{32,40},{40,48},{48,56},{56,64},{64,7... | collective-permute-start | bytes 393224 | tf_op jit(solution)/shard_map/while/body/eval_jaxpr/ppermute | solution.py:31
  481.2 8.1 %collective-permute-start = (f32[4,64,128]{2,1,0:T(8,128)S(1)}, f32[4,64,128]{2,1,0:T(8,128)S(1)}, u32[]{:S(2)}, u32[]{:S(2)}) collective-permute-start(f32[4,64,128]{2,1,0:T(8,128)S(1)} %fusion.82), channel_id=1, source_target_pairs={{0,8},{8,16},{16,24},{24,32},{32,40},{40,48},{48,56},{56,64},{64,7... | collective-permute-start | bytes 393224 | tf_op jit(solution)/shard_map/while/body/eval_jaxpr/ppermute | solution.py:31
  481.6 9.1 %collective-permute-start.1 = (f32[4,64,128]{2,1,0:T(8,128)S(1)}, f32[4,64,128]{2,1,0:T(8,128)S(1)}, u32[]{:S(2)}, u32[]{:S(2)}) collective-permute-start(f32[4,64,128]{2,1,0:T(8,128)S(1)} %fusion.83), channel_id=1, source_target_pairs={{0,8},{8,16},{16,24},{24,32},{32,40},{40,48},{48,56},{56,64},{64,7... | collective-permute-start | bytes 393224 | tf_op jit(solution)/shard_map/while/body/eval_jaxpr/ppermute | solution.py:31
  494.2 8.1 %collective-permute-start = (f32[4,64,128]{2,1,0:T(8,128)S(1)}, f32[4,64,128]{2,1,0:T(8,128)S(1)}, u32[]{:S(2)}, u32[]{:S(2)}) collective-permute-start(f32[4,64,128]{2,1,0:T(8,128)S(1)} %fusion.82), channel_id=1, source_target_pairs={{0,8},{8,16},{16,24},{24,32},{32,40},{40,48},{48,56},{56,64},{64,7... | collective-permute-start | bytes 393224 | tf_op jit(solution)/shard_map/while/body/eval_jaxpr/ppermute | solution.py:31
  494.6 9.1 %collective-permute-start.1 = (f32[4,64,128]{2,1,0:T(8,128)S(1)}, f32[4,64,128]{2,1,0:T(8,128)S(1)}, u32[]{:S(2)}, u32[]{:S(2)}) collective-permute-start(f32[4,64,128]{2,1,0:T(8,128)S(1)} %fusion.83), channel_id=1, source_target_pairs={{0,8},{8,16},{16,24},{24,32},{32,40},{40,48},{48,56},{56,64},{64,7... | collective-permute-start | bytes 393224 | tf_op jit(solution)/shard_map/while/body/eval_jaxpr/ppermute | solution.py:31
  507.2 8.1 %collective-permute-start = (f32[4,64,128]{2,1,0:T(8,128)S(1)}, f32[4,64,128]{2,1,0:T(8,128)S(1)}, u32[]{:S(2)}, u32[]{:S(2)}) collective-permute-start(f32[4,64,128]{2,1,0:T(8,128)S(1)} %fusion.82), channel_id=1, source_target_pairs={{0,8},{8,16},{16,24},{24,32},{32,40},{40,48},{48,56},{56,64},{64,7... | collective-permute-start | bytes 393224 | tf_op jit(solution)/shard_map/while/body/eval_jaxpr/ppermute | solution.py:31
  507.6 9.1 %collective-permute-start.1 = (f32[4,64,128]{2,1,0:T(8,128)S(1)}, f32[4,64,128]{2,1,0:T(8,128)S(1)}, u32[]{:S(2)}, u32[]{:S(2)}) collective-permute-start(f32[4,64,128]{2,1,0:T(8,128)S(1)} %fusion.83), channel_id=1, source_target_pairs={{0,8},{8,16},{16,24},{24,32},{32,40},{40,48},{48,56},{56,64},{64,7... | collective-permute-start | bytes 393224 | tf_op jit(solution)/shard_map/while/body/eval_jaxpr/ppermute | solution.py:31
  520.2 8.1 %collective-permute-start = (f32[4,64,128]{2,1,0:T(8,128)S(1)}, f32[4,64,128]{2,1,0:T(8,128)S(1)}, u32[]{:S(2)}, u32[]{:S(2)}) collective-permute-start(f32[4,64,128]{2,1,0:T(8,128)S(1)} %fusion.82), channel_id=1, source_target_pairs={{0,8},{8,16},{16,24},{24,32},{32,40},{40,48},{48,56},{56,64},{64,7... | collective-permute-start | bytes 393224 | tf_op jit(solution)/shard_map/while/body/eval_jaxpr/ppermute | solution.py:31
  520.6 9.1 %collective-permute-start.1 = (f32[4,64,128]{2,1,0:T(8,128)S(1)}, f32[4,64,128]{2,1,0:T(8,128)S(1)}, u32[]{:S(2)}, u32[]{:S(2)}) collective-permute-start(f32[4,64,128]{2,1,0:T(8,128)S(1)} %fusion.83), channel_id=1, source_target_pairs={{0,8},{8,16},{16,24},{24,32},{32,40},{40,48},{48,56},{56,64},{64,7... | collective-permute-start | bytes 393224 | tf_op jit(solution)/shard_map/while/body/eval_jaxpr/ppermute | solution.py:31
  533.5 9.1 %collective-permute-start.1 = (f32[4,64,128]{2,1,0:T(8,128)S(1)}, f32[4,64,128]{2,1,0:T(8,128)S(1)}, u32[]{:S(2)}, u32[]{:S(2)}) collective-permute-start(f32[4,64,128]{2,1,0:T(8,128)S(1)} %fusion.83), channel_id=1, source_target_pairs={{0,8},{8,16},{16,24},{24,32},{32,40},{40,48},{48,56},{56,64},{64,7... | collective-permute-start | bytes 393224 | tf_op jit(solution)/shard_map/while/body/eval_jaxpr/ppermute | solution.py:31
  546.5 9.1 %collective-permute-start.1 = (f32[4,64,128]{2,1,0:T(8,128)S(1)}, f32[4,64,128]{2,1,0:T(8,128)S(1)}, u32[]{:S(2)}, u32[]{:S(2)}) collective-permute-start(f32[4,64,128]{2,1,0:T(8,128)S(1)} %fusion.83), channel_id=1, source_target_pairs={{0,8},{8,16},{16,24},{24,32},{32,40},{40,48},{48,56},{56,64},{64,7... | collective-permute-start | bytes 393224 | tf_op jit(solution)/shard_map/while/body/eval_jaxpr/ppermute | solution.py:31
  559.5 9.1 %collective-permute-start.1 = (f32[4,64,128]{2,1,0:T(8,128)S(1)}, f32[4,64,128]{2,1,0:T(8,128)S(1)}, u32[]{:S(2)}, u32[]{:S(2)}) collective-permute-start(f32[4,64,128]{2,1,0:T(8,128)S(1)} %fusion.83), channel_id=1, source_target_pairs={{0,8},{8,16},{16,24},{24,32},{32,40},{40,48},{48,56},{56,64},{64,7... | collective-permute-start | bytes 393224 | tf_op jit(solution)/shard_map/while/body/eval_jaxpr/ppermute | solution.py:31
  572.5 9.1 %collective-permute-start.1 = (f32[4,64,128]{2,1,0:T(8,128)S(1)}, f32[4,64,128]{2,1,0:T(8,128)S(1)}, u32[]{:S(2)}, u32[]{:S(2)}) collective-permute-start(f32[4,64,128]{2,1,0:T(8,128)S(1)} %fusion.83), channel_id=1, source_target_pairs={{0,8},{8,16},{16,24},{24,32},{32,40},{40,48},{48,56},{56,64},{64,7... | collective-permute-start | bytes 393224 | tf_op jit(solution)/shard_map/while/body/eval_jaxpr/ppermute | solution.py:31
  585.4 9.1 %collective-permute-start.1 = (f32[4,64,128]{2,1,0:T(8,128)S(1)}, f32[4,64,128]{2,1,0:T(8,128)S(1)}, u32[]{:S(2)}, u32[]{:S(2)}) collective-permute-start(f32[4,64,128]{2,1,0:T(8,128)S(1)} %fusion.83), channel_id=1, source_target_pairs={{0,8},{8,16},{16,24},{24,32},{32,40},{40,48},{48,56},{56,64},{64,7... | collective-permute-start | bytes 393224 | tf_op jit(solution)/shard_map/while/body/eval_jaxpr/ppermute | solution.py:31
  598.0 8.1 %collective-permute-start = (f32[4,64,128]{2,1,0:T(8,128)S(1)}, f32[4,64,128]{2,1,0:T(8,128)S(1)}, u32[]{:S(2)}, u32[]{:S(2)}) collective-permute-start(f32[4,64,128]{2,1,0:T(8,128)S(1)} %fusion.82), channel_id=1, source_target_pairs={{0,8},{8,16},{16,24},{24,32},{32,40},{40,48},{48,56},{56,64},{64,7... | collective-permute-start | bytes 393224 | tf_op jit(solution)/shard_map/while/body/eval_jaxpr/ppermute | solution.py:31
  598.4 9.1 %collective-permute-start.1 = (f32[4,64,128]{2,1,0:T(8,128)S(1)}, f32[4,64,128]{2,1,0:T(8,128)S(1)}, u32[]{:S(2)}, u32[]{:S(2)}) collective-permute-start(f32[4,64,128]{2,1,0:T(8,128)S(1)} %fusion.83), channel_id=1, source_target_pairs={{0,8},{8,16},{16,24},{24,32},{32,40},{40,48},{48,56},{56,64},{64,7... | collective-permute-start | bytes 393224 | tf_op jit(solution)/shard_map/while/body/eval_jaxpr/ppermute | solution.py:31
  608.3 11.0 %all-to-all-start.3 = ((bf16[4,64,128]{2,0,1:T(4,128)(2,1)}), bf16[4,64,128]{2,0,1:T(4,128)(2,1)S(1)}, u32[]{:S(2)}, u32[]{:S(2)}) async-start(bf16[4,64,128]{2,0,1:T(4,128)(2,1)} %copy.80), calls=%async_computation.3 | async-start | bytes 131072 | tf_op jit(solution)/shard_map/all_to_all | solution.py:162
  619.3 10.6 %all-to-all-start.2 = ((bf16[4,64,128]{2,0,1:T(4,128)(2,1)}), bf16[4,64,128]{2,0,1:T(4,128)(2,1)S(1)}, u32[]{:S(2)}, u32[]{:S(2)}) async-start(bf16[4,64,128]{2,0,1:T(4,128)(2,1)} %copy.81), calls=%async_computation.2 | async-start | bytes 131072 | tf_op jit(solution)/shard_map/all_to_all | solution.py:161
  629.9 11.6 %all-to-all-start.1 = ((bf16[4,64,1024]{2,0,1:T(4,128)(2,1)}), bf16[4,64,1024]{2,0,1:T(4,128)(2,1)S(1)}, u32[]{:S(2)}, u32[]{:S(2)}) async-start(bf16[4,64,1024]{2,0,1:T(4,128)(2,1)} %reshape.196), calls=%async_computation.1 | async-start | bytes 1048576 | tf_op jit(solution)/shard_map/all_to_all | solution.py:160
  (13 other events, 190.0 us)
Sparse Core Ops, SparseCore 0:
  10.8 88.4 all-gather.3
